TPU v7x, 512 devices: a whole 4x4x16 slice. The times are simulated.
512 devices in a mesh: blk: 64 (over z_lo, x, core), feat: 8 (over z_hi, y).
Axes of the slice: x: 4, y: 4, z: 16 (z_hi: 2, z_lo: 8; z = z_hi * 8 + z_lo), core: 2. Of those that a mesh axis runs over, the one named last changes fastest.
Arguments:
- grads: bfloat16 [32768, 16384], P('blk', 'feat'), may hold values from -6 to 6
- basis_left: float32 [8, 16, 16], P('feat'), may hold values from -1.5 to 1.5
- basis_right: float32 [8, 128, 128], P('feat'), may hold values from -0.5 to 0.5
- eigen: float32 [16384], P('feat'), may hold values from 0.05 to 20
- partner: int32 [1, 64], replicated, may hold values from 0 to 63, as said below
Outputs:
- tiles: float32 [1, 32768, 512], P(None, 'blk', 'feat')
Inputs may be any that keep to these rules, and one draw needn't show every extreme that they name: In every round partner[r, b] = b xor 2^k_r, one bit k_r per round, distinct between rounds; so the partners form a perfect matching.
All inputs are finite; a program needn't handle non-finite values.
Results may differ from a plain program's by a relative error of at most 0.0029.
Values may be sent and summed in bfloat16 or wider, within the bound.
No kernel may reach another device: no remote copies, remote signals or barrier semaphores. Data moves between devices by JAX's collectives and lax.ppermute only.
A program may use at most 64 MiB of HBM per device.

v0:
```python
import math

import jax
import jax.numpy as jnp
from jax import lax
from jax.sharding import PartitionSpec as P

F = 16384


precision_high = lax.Precision.HIGHEST


def for_sending(x):
    return jax.tree.map(lambda a: a.astype(jnp.bfloat16) if a.dtype == jnp.float32 else a, x)


def from_partner(block, axis, stride):
    count = lax.axis_size(axis)
    route = []
    for low in range(count):
        high = low | 1 << stride
        if high != low and high < count:
            route += [(low, high), (high, low)]
    return lax.ppermute(block, axis, route)


def precondition(rows, basis_left, basis_right, eigen):
    row_count = rows.shape[0]
    layer_count = basis_left.shape[0]
    reshaped = rows.astype(jnp.float32).reshape(
        row_count, layer_count, basis_left.shape[1], basis_right.shape[1]
    )
    damped = eigen.reshape(layer_count, basis_left.shape[1], basis_right.shape[1]) + 0.1
    sectioned = jnp.einsum("elab,lbd->elad", reshaped, basis_right, precision=precision_high)
    rotated = (
        jnp.einsum("elad,lac->elcd", sectioned, basis_left, precision=precision_high) / damped[None]
    )
    sectioned = jnp.einsum("elcd,lac->elad", rotated, basis_left, precision=precision_high)
    restored = jnp.einsum("elad,lbd->elab", sectioned, basis_right, precision=precision_high)
    return restored.reshape(row_count, -1).astype(jnp.bfloat16)


def precondition_blocked(grads, basis_left, basis_right, eigen):
    row_count = grads.shape[0]
    block_rows = math.gcd(row_count, 256)
    pieces = grads.reshape(row_count // block_rows, block_rows, grads.shape[1])
    done = lax.map(lambda piece: precondition(piece, basis_left, basis_right, eigen), pieces)
    return done.reshape(row_count, grads.shape[1])


def swap_level(block, level):
    return jax.tree.map(
        lambda part, own: part.astype(own.dtype),
        from_partner(for_sending(block), "blk", level),
        block,
    )


def body(grads, basis_left, basis_right, eigen, partner):
    owner_id = lax.axis_index("blk")
    levels = lax.axis_size("blk").bit_length() - 1
    scaling = 1.0 / jnp.sqrt(jnp.float32(F))
    row_count = grads.shape[0]
    share_cols = row_count // lax.axis_size("feat")
    opposite = partner[0, owner_id]
    round_mask = partner[0, 0]
    level_index = jnp.int32(0)
    for level in range(levels):
        level_index = level_index + level * jnp.bitwise_and(jnp.right_shift(round_mask, level), 1)
    is_lower = owner_id < opposite
    outgoing = lax.cond(
        is_lower, lambda: precondition_blocked(grads, basis_left, basis_right, eigen), lambda: grads
    )
    branches = [lambda source, chosen=level: swap_level(source, chosen) for level in range(levels)]
    incoming = lax.switch(level_index, branches, outgoing)
    partial_tile = (
        lax.dot_general(
            outgoing, incoming, (((1,), (1,)), ((), ())), preferred_element_type=jnp.float32
        )
        * scaling
    )
    summed = lax.psum(partial_tile, "feat")
    column_start = lax.axis_index("feat") * share_cols
    results = [lax.dynamic_slice_in_dim(summed, column_start, share_cols, 1)]
    return jnp.stack(results)


def solution(mesh):
    placed = (P("blk", "feat"), P("feat", None, None), P("feat", None, None), P("feat"), P())
    return jax.shard_map(
        body, mesh=mesh, in_specs=placed, out_specs=P(None, "blk", "feat"), check_vma=False
    )
```

profile of v0, /device:TPU:24, one launch (start us, length us, event | category | flops | bytes accessed | tf_op | source)
XLA Modules:
  0.0 326.5 jit_solution(17676777809322583323)
XLA Ops:
  6.6 3.2 copy.46
  14.2 24.7 %conditional.2 = (bf16[512,2048]{1,0:T(8,128)(2,1)}) conditional(s32[]{:T(128)} %convert_element_type.26, bf16[512,2048]{1,0:T(8,128)(2,1)} %copy.46, (bf16[512,2048]{1,0:T(8,128)(2,1)}, f32[1,128,128]{2,1,0:T(8,128)S(1)}, f32[1,16,16]{2,1,0:T(8,128)S(1)}, f32[2048]{0:T(1024)S(1)}) %tuple.58), branch_computations={%region_0.0_spmd, %region_1.4_spmd} | conditional | flops 1812989952 | bytes 27421336 | solution.py:72
  14.2 21.5 %while.9 = (s32[]{:T(128)}, bf16[2,256,2048]{2,1,0:T(8,128)(2,1)}, bf16[2,256,2048]{2,1,0:T(8,128)(2,1)}, f32[1,128,128]{2,1,0:T(8,128)S(1)}, f32[1,16,16]{2,1,0:T(8,128)S(1)}, /*index=5*/f32[2048]{0:T(1024)S(1)}, s32[]{:T(128)}) while((s32[]{:T(128)}, bf16[2,256,2048]{2,1,0:T(8,128)(2,1)}, bf16[2,256,2048]{2,1,0:T(8,128)(2,1)}, ...), condition=%wide.region_3.3_spmd, body=%wide.region_2.2_spmd.sunk | while | flops 1812989952 | bytes 23226960 | solution.py:48
  14.2 1.3 dynamic-slice_bitcast_fusion.3
  15.8 1.0 fusion.42
  16.8 1.9 fusion.43
  18.7 2.0 fusion.44
  20.6 2.6 fusion.45
  23.2 0.6 copy.26
  23.9 1.1 constant_dynamic-update-slice_fusion.2
  25.0 1.3 dynamic-slice_bitcast_fusion.3
  26.5 1.0 fusion.42
  27.5 1.9 fusion.43
  29.4 2.0 fusion.44
  31.4 2.6 fusion.45
  34.0 0.6 copy.26
  34.6 1.1 constant_dynamic-update-slice_fusion.2
  35.7 3.2 copy.35
  38.9 95.4 %conditional.3 = (bf16[512,2048]{1,0:T(8,128)(2,1)}) conditional(s32[]{:T(128)} %bitcast.21, bf16[512,2048]{1,0:T(8,128)(2,1)} %get-tuple-element.144, bf16[512,2048]{1,0:T(8,128)(2,1)} %get-tuple-element.144, bf16[512,2048]{1,0:T(8,128)(2,1)} %get-tuple-element.144, ...), branch_computations={%region_4.5_spmd, %region_5.6_spmd, %region_6.7_spmd, %region_7.8_... | conditional | bytes 8388656 | solution.py:76
  38.9 1.9 collective-permute-start.4
  40.8 93.5 %collective-permute-done.4 = bf16[512,2048]{1,0:T(8,128)(2,1)} collective-permute-done((bf16[512,2048]{1,0:T(8,128)(2,1)}, bf16[512,2048]{1,0:T(8,128)(2,1)}, u32[]{:S(2)}, u32[]{:S(2)}) %collective-permute-start.4) | collective-permute-done | bytes 2097184 | tf_op jit(solution)/shard_map/cond/branch_4_fun/ppermute | solution.py:25
  134.3 4.5 %convolution_multiply_fusion = f32[512,512]{0,1:T(8,128)} fusion(bf16[512,2048]{1,0:T(8,128)(2,1)} %get-tuple-element.144, bf16[512,2048]{1,0:T(8,128)(2,1)} %get-tuple-element.145), kind=kOutput, calls=%fused_computation.17 | convolution fusion | flops 1074003968 | bytes 5242880 | tf_op jit(solution)/shard_map/dot_general | solution.py:78
  138.8 179.2 %all-reduce.2.cloned.1.call-done = f32[512,512]{0,1:T(8,128)} async-done(((f32[512,512]{0,1:T(8,128)}), f32[512,512]{0,1:T(8,128)}) %all-reduce.2.cloned.1.call-update) | async-done | bytes 1048592 | tf_op jit(solution)/shard_map/psum | solution.py:83
  318.1 1.6 dynamic-slice_bitcast_fusion.1
  (16 shorter events, 1.1 us)
Async XLA Ops:
  6.5 7.6 %copy-start.1 = (f32[1,16,16]{2,1,0:T(8,128)S(1)}, f32[1,16,16]{2,1,0:T(8,128)}, u32[]{:S(2)}) copy-start(f32[1,16,16]{2,1,0:T(8,128)} %param.16) | copy-start | bytes 3076
  6.5 7.6 %copy-start = (f32[1,128,128]{2,1,0:T(8,128)S(1)}, f32[1,128,128]{2,1,0:T(8,128)}, u32[]{:S(2)}) copy-start(f32[1,128,128]{2,1,0:T(8,128)} %param.17) | copy-start | bytes 196612
  6.5 7.7 %copy-start.2 = (f32[2048]{0:T(1024)S(1)}, f32[2048]{0:T(1024)}, u32[]{:S(2)}) copy-start(f32[2048]{0:T(1024)} %param.18) | copy-start | bytes 24580
  6.5 3.2 copy-start.3
  6.5 311.5 %all-reduce.2.cloned.1.call-start = ((), (), s32[]{:S(2)}) async-start(), calls=%async_computation | async-start | bytes 2097152 | tf_op jit(solution)/shard_map/psum | solution.py:83
  38.9 95.4 %collective-permute-start.4 = (bf16[512,2048]{1,0:T(8,128)(2,1)}, bf16[512,2048]{1,0:T(8,128)(2,1)}, u32[]{:S(2)}, u32[]{:S(2)}) collective-permute-start(bf16[512,2048]{1,0:T(8,128)(2,1)} %param.8), channel_id=1, source_target_pairs={{0,128},{128,0},{8,136},{136,8},{16,144},{144,16},{24,152},{152,24... | collective-permute-start | bytes 6291464 | tf_op jit(solution)/shard_map/cond/branch_4_fun/ppermute | solution.py:25
Sparse Core Ops, SparseCore 0:
  139.0 179.0 all-reduce.1
where the time goes:
time: 327 us; the launch traced here: 326 us
  waiting for transfers between devices  273 us (83%)
  matrix products  19.3 us (6%)
  between operations  17.2 us (5%)
  local copies, waits for them, and re-layouts  15.1 us (5%)
    psum x1, waiting for transfers between devices, body(): summed = lax.psum(partial_tile, 'feat')  179 us
    ppermute x1, waiting for transfers between devices, from_partner(): return lax.ppermute(block, axis, route)  93.5 us
  transfers between devices with their start and end apart: 2, of which 2 were waited for; matrix products, arithmetic and copies ran while one was open for 0% of the time, Pallas kernels for 0%

commit v1 on v0

v1 whole, which is shorter than its diff:
```python
import functools

import jax
import jax.numpy as jnp
from jax import lax
from jax.experimental import pallas as pl
from jax.experimental.pallas import tpu as pltpu
from jax.sharding import PartitionSpec as P

FEATURES = 16384
FA = 16
FB = 128
ROWS = 512
COLS = FA * FB
WIDE = 16 * FA
Y_GROUPS = [[0, 1, 2, 3], [4, 5, 6, 7]]
VMEM = pl.BlockSpec(memory_space=pltpu.VMEM)
SMEM = pl.BlockSpec(memory_space=pltpu.SMEM)
f32, bf16 = jnp.float32, jnp.bfloat16


def split(v):
    high = v.astype(bf16)
    return high, (v - high.astype(f32)).astype(bf16)


def dot(a, b):
    return jnp.dot(a, b, preferred_element_type=f32)


def dot_t(a, b):
    return lax.dot_general(a, b, (((1,), (1,)), ((), ())), preferred_element_type=f32)


def prepare(left, right, damped, lt, l, rs, rr, inv):
    spread = (
        lax.broadcasted_iota(jnp.int32, (WIDE, FA), 0) >> 4
        == lax.broadcasted_iota(jnp.int32, (WIDE, FA), 1)
    ).astype(bf16)
    same = (lax.broadcasted_iota(jnp.int32, (WIDE, WIDE), 0) & 15) == (
        lax.broadcasted_iota(jnp.int32, (WIDE, WIDE), 1) & 15
    )
    for k, v in enumerate(split(left[...])):
        wide = dot_t(dot(spread, v).astype(bf16), spread)
        l[k] = jnp.where(same, wide, 0.0).astype(bf16)
        wide = dot_t(dot_t(spread, v).astype(bf16), spread)
        lt[k] = jnp.where(same, wide, 0.0).astype(bf16)
    basis = right[...]
    for k, v in enumerate(split(basis)):
        rs[:, k * FB : (k + 1) * FB] = v
    for k, v in enumerate(split(basis.T)):
        rr[:FB, k * FB : (k + 1) * FB] = v
        rr[FB:, k * FB : (k + 1) * FB] = v
    reciprocal = 1.0 / (damped[...] + 0.1)
    inv[...] = jnp.broadcast_to(reciprocal[:, None, :], (FA, 16, FB)).reshape(WIDE, FB)


PREPARED = (
    jax.ShapeDtypeStruct((2, WIDE, WIDE), bf16),
    jax.ShapeDtypeStruct((2, WIDE, WIDE), bf16),
    jax.ShapeDtypeStruct((FB, 2 * FB), bf16),
    jax.ShapeDtypeStruct((2 * FB, 2 * FB), bf16),
    jax.ShapeDtypeStruct((WIDE, FB), f32),
)


def prepared(left, right, damped):
    return pl.pallas_call(
        prepare, out_shape=PREPARED, in_specs=[VMEM] * 3, out_specs=[VMEM] * 5, name="prepare"
    )(left, right, damped)


def halves(v):
    return v[:, :FB] + v[:, FB:]


def precondition(x, out, lt, l, rs, rr, inv):
    def group(g, carry):
        at = pl.ds(pl.multiple_of(g * 16, 16), 16)
        z = jnp.concatenate([x[at, a * FB : (a + 1) * FB] for a in range(FA)], axis=0)
        v = halves(dot(z, rs[...]))
        high, low = split(v)
        v = halves(dot(lt[0], jnp.concatenate([high, low], axis=1))) + dot(lt[1], high)
        high, low = split(v * inv[...])
        v = halves(dot(l[0], jnp.concatenate([high, low], axis=1))) + dot(l[1], high)
        high, low = split(v)
        v = halves(dot(jnp.concatenate([high, low], axis=1), rr[...])).astype(bf16)
        for a in range(FA):
            out[at, a * FB : (a + 1) * FB] = v[a * 16 : (a + 1) * 16]
        return carry

    lax.fori_loop(0, x.shape[0] // 16, group, 0, unroll=2)


def own_kernel(lower, x, lt, l, rs, rr, inv, out):
    @pl.when(lower[0] == 1)
    def _():
        precondition(x, out, lt, l, rs, rr, inv)

    @pl.when(lower[0] == 0)
    def _():
        out[...] = x[...]


def whole(a):
    return pl.BlockSpec(a.shape, lambda i: (0,) * len(a.shape))


def own_side(lower, x, ready, step=128):
    rows = pl.BlockSpec((step, COLS), lambda i: (i, 0))
    return pl.pallas_call(
        own_kernel,
        grid=(x.shape[0] // step,),
        out_shape=jax.ShapeDtypeStruct(x.shape, bf16),
        in_specs=[SMEM, rows] + [whole(a) for a in ready],
        out_specs=rows,
        name="own",
    )(lower, x, *ready)


def tile_kernel(lower, y, own, lt, l, rs, rr, inv, out, held):
    @pl.when(lower[0] == 1)
    def _():
        out[0, 0] = dot_t(y[...], own[...]) * (1.0 / 128.0)

    @pl.when(lower[0] == 0)
    def _():
        precondition(y, held, lt, l, rs, rr, inv)
        out[0, 0] = dot_t(held[...], own[...]) * (1.0 / 128.0)


def tile_side(lower, y, own, ready):
    step = y.shape[0] // 8
    return pl.pallas_call(
        tile_kernel,
        grid=(8,),
        out_shape=jax.ShapeDtypeStruct((4, 2, step, ROWS), f32),
        in_specs=[SMEM, pl.BlockSpec((step, COLS), lambda i: (i, 0)), whole(own)]
        + [whole(a) for a in ready],
        out_specs=pl.BlockSpec((1, 1, step, ROWS), lambda i: (i % 4, i // 4, 0, 0)),
        scratch_shapes=[pltpu.VMEM((step, COLS), bf16)],
        name="tile",
    )(lower, y, own, *ready)


def fold_kernel(z_hi, parts, keep, send):
    z = z_hi[0]
    keep[...] = parts[0, z] + parts[1, z] + parts[2, z] + parts[3, z]
    o = 1 - z
    send[...] = (parts[0, o] + parts[1, o] + parts[2, o] + parts[3, o]).astype(send.dtype)


def fold(z_hi, parts):
    shape = parts.shape[2:]
    return pl.pallas_call(
        fold_kernel,
        out_shape=(jax.ShapeDtypeStruct(shape, f32), jax.ShapeDtypeStruct(shape, f32)),
        in_specs=[SMEM, VMEM],
        out_specs=(VMEM, VMEM),
        name="fold",
    )(z_hi, parts)


def summed(z_hi, tile):
    parts = lax.all_to_all(tile, "feat", 0, 0, axis_index_groups=Y_GROUPS)
    keep, send = fold(z_hi, parts)
    return keep + lax.ppermute(send, "feat", [(f, f ^ 4) for f in range(8)])


def swap(level, x):
    return lax.ppermute(x, "blk", [(b, b ^ (1 << level)) for b in range(64)])


def plain(level, x, ready, lower, z_hi):
    incoming = swap(level, x)
    own = own_side(lower, x, ready)
    return summed(z_hi, tile_side(lower, incoming, own, ready))


def body(grads, basis_left, basis_right, eigen, partner):
    mask = partner[0, 0]
    lower = (jnp.bitwise_and(lax.axis_index("blk"), mask) == 0).astype(jnp.int32).reshape(1)
    z_hi = (lax.axis_index("feat") // 4).astype(jnp.int32).reshape(1)
    level = sum((mask >= 1 << k).astype(jnp.int32) for k in range(1, 6))
    ready = prepared(basis_left[0], basis_right[0], eigen.reshape(FA, FB))
    branches = [functools.partial(plain, k) for k in range(6)]
    out = lax.switch(level, branches, grads, ready, lower, z_hi)
    return out.T[None]


def solution(mesh):
    placed = (P("blk", "feat"), P("feat", None, None), P("feat", None, None), P("feat"), P())
    return jax.shard_map(
        body, mesh=mesh, in_specs=placed, out_specs=P(None, "blk", "feat"), check_vma=False
    )
```

time: 327 us -> 132 us (0.40)
  the two profiles are of different devices: /device:TPU:24 before, /device:TPU:34 now
where the time goes in v1:
time: 132 us
  waiting for transfers between devices  52 us (39%)
  Pallas kernels  35 us (27%)
  blocking collectives  18.8 us (14%)
  starting transfers between devices  17.3 us (13%)
  between operations  3.9 us (3%)
  local copies, waits for them, and re-layouts  3.15 us (2%)
  other arithmetic  1.58 us (1%)
    ppermute x1, waiting for transfers between devices, swap(): return lax.ppermute(x, 'blk', [(b, b ^ 1 << level) for b in range(64)])  43.2 us
    pallas_call x1, Pallas kernels, tile_side(): pl.pallas_call(tile_kernel, grid=(8,), out_shape=jax.ShapeDtypeStruct((4,...  27.9 us
    all_to_all x1, blocking collectives, summed(): parts = lax.all_to_all(tile, 'feat', 0, 0, axis_index_groups=Y_GROUPS)  18.8 us
    ppermute x1, starting transfers between devices, summed(): return keep + lax.ppermute(send, 'feat', [(f, f ^ 4) for f in range(8)])  14.8 us
    ppermute x1, waiting for transfers between devices, summed(): return keep + lax.ppermute(send, 'feat', [(f, f ^ 4) for f in range(8)])  8.85 us
    pallas_call x1, Pallas kernels, own_side(): pl.pallas_call(own_kernel, grid=(x.shape[0] // step,), out_shape=jax.Shap...  3.82 us
    cond x4, local copies, waits for them, and re-layouts  3.15 us
  transfers between devices with their start and end apart: 2, of which 2 were waited for; matrix products, arithmetic and copies ran while one was open for 1% of the time, Pallas kernels for 3%

profile of v1, /device:TPU:34, one launch (start us, length us, event | category | flops | bytes accessed | tf_op | source)
XLA Modules:
  0.0 131.8 jit_solution(17746555646989115292)
XLA Ops:
  3.9 1.4 %prepare.1 = (bf16[2,256,256]{2,1,0:T(8,128)(2,1)S(1)}, bf16[2,256,256]{2,1,0:T(8,128)(2,1)S(1)}, bf16[128,256]{1,0:T(8,128)(2,1)S(1)}, bf16[256,256]{1,0:T(8,128)(2,1)S(1)}, f32[256,128]{1,0:T(8,128)S(1)}) custom-call(f32[16,16]{1,0:T(8,128)} %bitcast.12, f32[128,128]{1,0:T(8,128)} %bitcast.11, f32[16,128]{1,0:T(8,128)} %bitcast.13), custom_call_target="tpu_custom_call" | custom-call | tf_op jit(solution)/shard_map/prepare/pallas_call | solution.py:68
  5.3 124.9 %conditional.1 = (f32[64,512]{1,0:T(8,128)}, f32[64,512]{1,0:T(8,128)}, f32[64,512]{1,0:T(8,128)}, f32[64,512]{1,0:T(8,128)S(1)}, f32[64,512]{1,0:T(8,128)S(1)}) conditional(s32[]{:T(128)} %clamp.3, (bf16[512,2048]{1,0:T(8,128)(2,1)}, s32[1]{0:T(128)}, bf16[2,256,256]{2,1,0:T(8,128)(2,1)S(1)}, ...), branch_computations={%region_0.1_spmd, %region_1.2_spmd, %region_2.3_spmd, %region_3.4_... | conditional | bytes 19923092 | solution.py:187
  5.3 2.4 %collective-permute-start.2 = (bf16[512,2048]{1,0:T(8,128)(2,1)}, bf16[512,2048]{1,0:T(8,128)(2,1)S(1)}, u32[]{:S(2)}, u32[]{:S(2)}) collective-permute-start(bf16[512,2048]{1,0:T(8,128)(2,1)} %get-tuple-element.117.x), channel_id=1, source_target_pairs={{0,16},{8,24},{16,0},{24,8},{32,48},{40,56},{48,32},{56,40},{64,80... | collective-permute-start | bytes 6291464 | tf_op jit(solution)/shard_map/cond/branch_1_fun/ppermute | solution.py:171
  7.8 3.8 %own.7 = bf16[512,2048]{1,0:T(8,128)(2,1)} custom-call(s32[1]{0:T(128)} %get-tuple-element.116.lower, bf16[512,2048]{1,0:T(8,128)(2,1)} %get-tuple-element.117.x, bf16[2,256,256]{2,1,0:T(8,128)(2,1)S(1)} %get-tuple-element.118.lt, bf16[2,256,256]{2,1,0:T(8,128)(2,1)S(1)} %get-tuple-element.119.l, bf16[128,256]{1,0:T(8,128)(2,1)S(1)} %get-tuple-element.120.rs, ...), custom_call_target="tpu_custom_call" | custom-call | tf_op jit(solution)/shard_map/cond/branch_1_fun/own/pallas_call | solution.py:111
  11.6 43.2 %collective-permute-done.2.y = bf16[512,2048]{1,0:T(8,128)(2,1)S(1)} collective-permute-done((bf16[512,2048]{1,0:T(8,128)(2,1)}, bf16[512,2048]{1,0:T(8,128)(2,1)S(1)}, u32[]{:S(2)}, u32[]{:S(2)}) %collective-permute-start.2) | collective-permute-done | bytes 2097184 | tf_op jit(solution)/shard_map/cond/branch_1_fun/ppermute | solution.py:171
  54.8 0.0 copy-start.1
  54.8 1.3 %copy-done.1 = bf16[512,2048]{1,0:T(8,128)(2,1)} copy-done((bf16[512,2048]{1,0:T(8,128)(2,1)}, bf16[512,2048]{1,0:T(8,128)(2,1)S(1)}, u32[]{:S(2)}) %copy-start.1) | copy-done | bytes 2097176 | tf_op jit(solution)/shard_map/cond
  56.1 27.9 %tile.7 = f32[4,2,64,512]{3,2,1,0:T(8,128)} custom-call(s32[1]{0:T(128)} %get-tuple-element.116.lower, bf16[512,2048]{1,0:T(8,128)(2,1)} %copy-done.1, bf16[512,2048]{1,0:T(8,128)(2,1)} %own.7, bf16[2,256,256]{2,1,0:T(8,128)(2,1)S(1)} %get-tuple-element.118.lt, bf16[2,256,256]{2,1,0:T(8,128)(2,1)S(1)} %get-tuple-element.119.l, ...), custom_call_target="tpu_custom_call" | custom-call | tf_op jit(solution)/shard_map/cond/branch_1_fun/tile/pallas_call | solution.py:134
  84.0 18.8 %all_to_all.25.parts = f32[4,2,64,512]{3,2,1,0:T(8,128)} all-to-all(f32[4,2,64,512]{3,2,1,0:T(8,128)} %tile.7), channel_id=1, replica_groups={{0,1,2,3},{4,5,6,7},{8,9,10,11},{12,13,14,15},{16,17,18,19},{20,21,22,2..., dimensions={0} | all-to-all | bytes 2097152 | tf_op jit(solution)/shard_map/cond/branch_1_fun/all_to_all | solution.py:165
  102.8 2.0 %fold.7 = (f32[64,512]{1,0:T(8,128)}, f32[64,512]{1,0:T(8,128)}) custom-call(s32[1]{0:T(128)} %get-tuple-element.115.z_hi, f32[4,2,64,512]{3,2,1,0:T(8,128)} %all_to_all.25.parts), custom_call_target="tpu_custom_call" | custom-call | tf_op jit(solution)/shard_map/cond/branch_1_fun/fold/pallas_call | solution.py:155
  104.7 14.8 %collective-permute-start.3 = (f32[64,512]{1,0:T(8,128)}, f32[64,512]{1,0:T(8,128)}, u32[]{:S(2)}, u32[]{:S(2)}) collective-permute-start(f32[64,512]{1,0:T(8,128)} %get-tuple-element.246), channel_id=1, source_target_pairs={{0,4},{1,5},{2,6},{3,7},{4,0},{5,1},{6,2},{7,3},{8,12},{9,13},{10,... | collective-permute-start | bytes 393224 | tf_op jit(solution)/shard_map/cond/branch_1_fun/ppermute | solution.py:167
  119.5 0.9 copy.39
  120.4 8.8 %collective-permute-done.3 = f32[64,512]{1,0:T(8,128)} collective-permute-done((f32[64,512]{1,0:T(8,128)}, f32[64,512]{1,0:T(8,128)}, u32[]{:S(2)}, u32[]{:S(2)}) %collective-permute-start.3) | collective-permute-done | bytes 131104 | tf_op jit(solution)/shard_map/cond/branch_1_fun/ppermute | solution.py:167
  129.3 0.9 copy.49
  130.2 1.6 %add_bitcast_fusion = f32[1,512,64]{1,2,0:T(8,128)} fusion(f32[64,512]{1,0:T(8,128)S(1)} %get-tuple-element.177, f32[64,512]{1,0:T(8,128)} %get-tuple-element.178), kind=kLoop, calls=%fused_computation | loop fusion | flops 32768 | bytes 393216 | tf_op jit(solution)/shard_map/broadcast_in_dim | solution.py:188
Async XLA Ops:
  5.3 49.5 %collective-permute-start.2 = (bf16[512,2048]{1,0:T(8,128)(2,1)}, bf16[512,2048]{1,0:T(8,128)(2,1)S(1)}, u32[]{:S(2)}, u32[]{:S(2)}) collective-permute-start(bf16[512,2048]{1,0:T(8,128)(2,1)} %get-tuple-element.117.x), channel_id=1, source_target_pairs={{0,16},{8,24},{16,0},{24,8},{32,48},{40,56},{48,32},{56,40},{64,80... | collective-permute-start | bytes 6291464 | tf_op jit(solution)/shard_map/cond/branch_1_fun/ppermute | solution.py:171
  54.8 1.3 %copy-start.1 = (bf16[512,2048]{1,0:T(8,128)(2,1)}, bf16[512,2048]{1,0:T(8,128)(2,1)S(1)}, u32[]{:S(2)}) copy-start(bf16[512,2048]{1,0:T(8,128)(2,1)S(1)} %collective-permute-done.2.y) | copy-start | bytes 6291460 | tf_op jit(solution)/shard_map/cond
  104.7 24.6 %collective-permute-start.3 = (f32[64,512]{1,0:T(8,128)}, f32[64,512]{1,0:T(8,128)}, u32[]{:S(2)}, u32[]{:S(2)}) collective-permute-start(f32[64,512]{1,0:T(8,128)} %get-tuple-element.246), channel_id=1, source_target_pairs={{0,4},{1,5},{2,6},{3,7},{4,0},{5,1},{6,2},{7,3},{8,12},{9,13},{10,... | collective-permute-start | bytes 393224 | tf_op jit(solution)/shard_map/cond/branch_1_fun/ppermute | solution.py:167

commit v2 on v1

v2 whole, which is shorter than its diff:
```python
import functools

import jax
import jax.numpy as jnp
from jax import lax
from jax.experimental import pallas as pl
from jax.experimental.pallas import tpu as pltpu
from jax.sharding import PartitionSpec as P

FA = 16
FB = 128
ROWS = 512
COLS = FA * FB
WIDE = 16 * FA
SHARE = 64
PAIRS = 4
SCALE = 1.0 / 128.0
Y_GROUPS = [[0, 1, 2, 3], [4, 5, 6, 7]]
VMEM = pl.BlockSpec(memory_space=pltpu.VMEM)
SMEM = pl.BlockSpec(memory_space=pltpu.SMEM)
ANY = pl.BlockSpec(memory_space=pl.ANY)
f32, bf16 = jnp.float32, jnp.bfloat16


def params(flops, moved):
    return dict(
        compiler_params=pltpu.CompilerParams(vmem_limit_bytes=28 << 20),
        cost_estimate=pl.CostEstimate(flops=flops, bytes_accessed=moved, transcendentals=0),
    )


def split(v):
    high = v.astype(bf16)
    return high, (v - high.astype(f32)).astype(bf16)


def dot(a, b):
    return jnp.dot(a, b, preferred_element_type=f32)


def dot_t(a, b):
    return lax.dot_general(a, b, (((1,), (1,)), ((), ())), preferred_element_type=f32)


def prepare(left, right, eigen, lt, l, rr, rrt, inv):
    spread = (
        lax.broadcasted_iota(jnp.int32, (WIDE, FA), 0) >> 4
        == lax.broadcasted_iota(jnp.int32, (WIDE, FA), 1)
    ).astype(bf16)
    same = (lax.broadcasted_iota(jnp.int32, (WIDE, WIDE), 0) & 15) == (
        lax.broadcasted_iota(jnp.int32, (WIDE, WIDE), 1) & 15
    )
    for k, v in enumerate(split(left[...])):
        wide = dot_t(dot(spread, v).astype(bf16), spread)
        l[k] = jnp.where(same, wide, 0.0).astype(bf16)
        wide = dot_t(dot_t(spread, v).astype(bf16), spread)
        lt[k] = jnp.where(same, wide, 0.0).astype(bf16)
    for out, basis in ((rr, right[...]), (rrt, right[...].T)):
        for k, v in enumerate(split(basis)):
            out[:FB, k * FB : (k + 1) * FB] = v
            out[FB:, k * FB : (k + 1) * FB] = v
    reciprocal = 1.0 / (eigen[...] + 0.1)
    inv[...] = jnp.broadcast_to(reciprocal[:, None, :], (FA, 16, FB)).reshape(WIDE, FB)


PREPARED = (
    jax.ShapeDtypeStruct((2, WIDE, WIDE), bf16),
    jax.ShapeDtypeStruct((2, WIDE, WIDE), bf16),
    jax.ShapeDtypeStruct((2 * FB, 2 * FB), bf16),
    jax.ShapeDtypeStruct((2 * FB, 2 * FB), bf16),
    jax.ShapeDtypeStruct((WIDE, FB), f32),
)


def prepared(left, right, eigen):
    return pl.pallas_call(
        prepare, out_shape=PREPARED, in_specs=[VMEM] * 3, out_specs=[VMEM] * 5, name="prepare"
    )(left, right, eigen)


def halves(v):
    return v[:, :FB] + v[:, FB:]


def beside(v):
    return jnp.concatenate([v[:WIDE], v[WIDE:]], axis=1)


def precondition(x, out, lt, l, rr, rrt, inv):
    def group(g, carry):
        spots = [
            [pl.ds(pl.multiple_of((g * PAIRS + q) * 32 + 16 * k, 16), 16) for k in range(2)]
            for q in range(PAIRS)
        ]
        values = []
        for two in spots:
            z = jnp.concatenate(
                [
                    jnp.concatenate([x[at, a * FB : (a + 1) * FB] for a in range(FA)], axis=0)
                    for at in two
                ],
                axis=1,
            )
            v = dot(lt[0], z) + dot(lt[1], z)
            values.append(jnp.concatenate([v[:, :FB], v[:, FB:]], axis=0))
        values = [halves(dot(jnp.concatenate(split(v), axis=1), rr[...])) for v in values]
        scale = jnp.concatenate([inv[...], inv[...]], axis=0)
        values = [v * scale for v in values]
        values = [halves(dot(jnp.concatenate(split(v), axis=1), rrt[...])) for v in values]
        for two, v in zip(spots, values):
            high, low = [beside(part) for part in split(v)]
            v = (dot(l[0], high) + dot(l[1], high) + dot(l[0], low)).astype(bf16)
            for k, at in enumerate(two):
                for a in range(FA):
                    out[at, a * FB : (a + 1) * FB] = v[
                        a * 16 : (a + 1) * 16, k * FB : (k + 1) * FB
                    ]
        return carry

    lax.fori_loop(0, x.shape[0] // (32 * PAIRS), group, 0)


def whole(a):
    return pl.BlockSpec(a.shape, lambda *_: (0,) * len(a.shape))


def own_kernel(lower, x, lt, l, rr, rrt, inv, out):
    @pl.when(lower[0] == 1)
    def _():
        precondition(x, out, lt, l, rr, rrt, inv)

    @pl.when(lower[0] == 0)
    def _():
        out[...] = x[...]


def own_side(lower, x, ready):
    rows = pl.BlockSpec((128, COLS), lambda i: (i, 0))
    return pl.pallas_call(
        own_kernel,
        grid=(ROWS // 128,),
        out_shape=jax.ShapeDtypeStruct(x.shape, bf16),
        in_specs=[SMEM, rows] + [whole(a) for a in ready],
        out_specs=rows,
        name="own",
        **params(5 << 30, 4 << 20),
    )(lower, x, *ready)


def piece_kernel(at, n, half, lower, x, *rest):
    out, sems = rest[-2:]
    columns = pl.ds(pl.multiple_of(lower[0] * (COLS // 2), COLS // 2), COLS // 2)
    copies = []
    for i in range(8):
        rows = pl.ds(((i % 2) * 4 + i // 2) * SHARE + at, n)
        source = x.at[rows, columns] if half else x.at[rows]
        copies.append(pltpu.make_async_copy(source, out.at[pl.ds(i * n, n)], sems.at[i]))
    for copy in copies:
        copy.start()
    for copy in copies:
        copy.wait()


def piece(lower, x, at, n, half, after=None):
    after = [] if after is None else [after]
    columns = COLS // 2 if half else COLS
    return pl.pallas_call(
        functools.partial(piece_kernel, at, n, half),
        out_shape=jax.ShapeDtypeStruct((8 * n, columns), bf16),
        in_specs=[SMEM, ANY] + [ANY] * len(after),
        out_specs=ANY,
        scratch_shapes=[pltpu.SemaphoreType.DMA((8,))],
        name="piece",
        **params(0, 2 * 8 * n * columns * 2),
    )(lower, x, *after)


def tile_kernel(raw, lower, y, own, *rest):
    if not raw:
        out = rest[-1]
        out[...] = dot_t(y[...], own[...]) * SCALE
        return
    ready, out, held = rest[:5], rest[-2], rest[-1]

    @pl.when(lower[0] == 1)
    def _():
        out[...] = dot_t(y[...], own[...]) * SCALE

    @pl.when(lower[0] == 0)
    def _():
        precondition(y, held, *ready)
        out[...] = dot_t(held[...], own[...]) * SCALE


def tile(raw, lower, y, own, ready, after=None):
    after = [] if after is None else [after]
    ready = ready if raw else ()
    out = pl.pallas_call(
        functools.partial(tile_kernel, raw),
        out_shape=jax.ShapeDtypeStruct((y.shape[0], ROWS), f32),
        in_specs=[SMEM, VMEM, VMEM] + [VMEM] * len(ready) + [ANY] * len(after),
        out_specs=VMEM,
        scratch_shapes=[pltpu.VMEM(y.shape, bf16)] if raw else [],
        name="tile",
        **params(2 * y.shape[0] * ROWS * COLS, 3 << 20),
    )(lower, y, own, *ready, *after)
    return out.reshape(4, 2, y.shape[0] // 8, ROWS)


def fold_kernel(z_hi, parts, keep, send):
    z = z_hi[0]
    keep[...] = parts[0, z] + parts[1, z] + parts[2, z] + parts[3, z]
    o = 1 - z
    send[...] = parts[0, o] + parts[1, o] + parts[2, o] + parts[3, o]


def fold(z_hi, parts):
    shape = jax.ShapeDtypeStruct(parts.shape[2:], f32)
    return pl.pallas_call(
        fold_kernel,
        out_shape=(shape, shape),
        in_specs=[SMEM, VMEM],
        out_specs=(VMEM, VMEM),
        name="fold",
        **params(0, 4 * parts.size),
    )(z_hi, parts)


def summed(z_hi, parts):
    parts = lax.all_to_all(parts, "feat", 0, 0, axis_index_groups=Y_GROUPS)
    keep, send = fold(z_hi, parts)
    return keep, lax.ppermute(send, "feat", [(f, f ^ 4) for f in range(8)])


def swap(level, x):
    return lax.ppermute(x, "blk", [(b, b ^ (1 << level)) for b in range(64)])


def join_kernel(*refs):
    out, at = refs[-1], 0
    for a, b in zip(refs[:-1:2], refs[1:-1:2]):
        out[at : at + a.shape[0]] = a[...] + b[...]
        at += a.shape[0]


def join(pieces):
    flat = [a for both in pieces for a in both]
    return pl.pallas_call(
        join_kernel,
        out_shape=jax.ShapeDtypeStruct((SHARE, ROWS), f32),
        in_specs=[VMEM] * len(flat),
        out_specs=VMEM,
        name="join",
        **params(0, 4 * SHARE * ROWS * 3),
    )(*flat)


def by_pieces(sizes, level, x, ready, lower, z_hi):
    own = own_side(lower, x, ready)
    done, at, arrived = [], 0, None
    for k, n in enumerate(sizes):
        arrived = swap(level, piece(lower, x if k == 0 else own, at, n, False, arrived))
        done.append(summed(z_hi, tile(k == 0, lower, arrived, own, ready)))
        at += n
    return join(done)


def half_kernel(n, lower, y, own, *rest):
    out = rest[-1]

    def both(mine):
        rows = dot_t(y[...], mine) * SCALE
        across = dot_t(mine, y[...]) * SCALE
        for i in range(8):
            out[i, :n] = rows[i * n : (i + 1) * n]
            first = ((i % 2) * 4 + i // 2) * SHARE
            for q in range(SHARE // n):
                out[i, n:, q * 8 * n : (q + 1) * 8 * n] = across[
                    first + q * n : first + (q + 1) * n
                ]

    @pl.when(lower[0] == 1)
    def _():
        both(own[:, : COLS // 2])

    @pl.when(lower[0] == 0)
    def _():
        both(own[:, COLS // 2 :])


def half_tile(n, lower, y, own, after=None):
    after = [] if after is None else [after]
    out = pl.pallas_call(
        functools.partial(half_kernel, n),
        out_shape=jax.ShapeDtypeStruct((8, 2 * n, ROWS), f32),
        in_specs=[SMEM, VMEM, VMEM] + [ANY] * len(after),
        out_specs=VMEM,
        name="half_tile",
        **params(4 * y.shape[0] * ROWS * COLS // 2, 3 << 20),
    )(lower, y, own, *after)
    return out.reshape(4, 2, 2 * n, ROWS)


def last_kernel(n, *refs):
    out, count = refs[-1], SHARE // n
    blocks = []
    for c in range(count):
        far = refs[3 * c + 2][...]
        blocks.append(
            jnp.concatenate([far[:, q * 8 * n : (q + 1) * 8 * n] for q in range(SHARE // n)], axis=0)
        )
    spread = []
    for f in range(8):
        i = (f % 4) * 2 + f // 4
        spread += [block[:, i * n : (i + 1) * n] for block in blocks]
    out[...] = jnp.concatenate(spread, axis=1)
    for c in range(count):
        out[c * n : (c + 1) * n] += refs[3 * c][:n] + refs[3 * c + 1][:n]


def last(n, pieces):
    flat = [a for three in pieces for a in three]
    return pl.pallas_call(
        functools.partial(last_kernel, n),
        out_shape=jax.ShapeDtypeStruct((SHARE, ROWS), f32),
        in_specs=[VMEM] * len(flat),
        out_specs=VMEM,
        name="last",
        **params(0, 4 * SHARE * ROWS * 6),
    )(*flat)


def by_halves(n, level, x, ready, lower, z_hi):
    own = own_side(lower, x, ready)
    done, arrived, kept = [], None, None
    for c in range(SHARE // n):
        arrived = swap(level, piece(lower, own, c * n, n, True, arrived))
        kept, got = summed(z_hi, half_tile(n, lower, arrived, own, kept))
        done.append((kept, got, swap(level, kept[n:] + got[n:])))
    return last(n, done)


PLANS = [
    functools.partial(by_pieces, (32, 32), 0),
    functools.partial(by_halves, 32, 1),
    functools.partial(by_halves, 32, 2),
    functools.partial(by_halves, 32, 3),
    functools.partial(by_halves, 16, 4),
    functools.partial(by_halves, 16, 5),
]


def body(grads, basis_left, basis_right, eigen, partner):
    mask = partner[0, 0]
    lower = (jnp.bitwise_and(lax.axis_index("blk"), mask) == 0).astype(jnp.int32).reshape(1)
    z_hi = (lax.axis_index("feat") // 4).astype(jnp.int32).reshape(1)
    level = sum((mask >= 1 << k).astype(jnp.int32) for k in range(1, 6))
    ready = prepared(basis_left[0], basis_right[0], eigen.reshape(FA, FB))
    out = lax.switch(level, PLANS, grads, ready, lower, z_hi)
    return out.T[None]


def solution(mesh):
    placed = (P("blk", "feat"), P("feat", None, None), P("feat", None, None), P("feat"), P())
    return jax.shard_map(
        body, mesh=mesh, in_specs=placed, out_specs=P(None, "blk", "feat"), check_vma=False
    )
```

time: 132 us -> 106 us (0.80)
  the two profiles are of different devices: /device:TPU:34 before, /device:TPU:24 now
where the time goes in v2:
time: 106 us; the launch traced here: 104 us
  starting transfers between devices  44.8 us (42%)
  waiting for transfers between devices  39.6 us (37%)
  Pallas kernels  13.7 us (13%)
  between operations  3.9 us (4%)
  local copies, waits for them, and re-layouts  2.06 us (2%)
    ppermute x2, starting transfers between devices, summed(): return (keep, lax.ppermute(send, 'feat', [(f, f ^ 4) for f in range(8)]))  26.4 us
    ppermute x4, waiting for transfers between devices, swap(): return lax.ppermute(x, 'blk', [(b, b ^ 1 << level) for b in range(64)])  22 us
    ppermute x2, waiting for transfers between devices, summed(): return (keep, lax.ppermute(send, 'feat', [(f, f ^ 4) for f in range(8)]))  9.59 us
    all_to_all x2, starting transfers between devices, summed(): parts = lax.all_to_all(parts, 'feat', 0, 0, axis_index_groups=Y_GROUPS)  9.48 us
    ppermute x4, starting transfers between devices, swap(): return lax.ppermute(x, 'blk', [(b, b ^ 1 << level) for b in range(64)])  8.83 us
    all_to_all x2, waiting for transfers between devices, summed(): parts = lax.all_to_all(parts, 'feat', 0, 0, axis_index_groups=Y_GROUPS)  7.99 us
    pallas_call x1, Pallas kernels, own_side(): pl.pallas_call(own_kernel, grid=(ROWS // 128,), out_shape=jax.ShapeDtypeS...  6.78 us
    pallas_call x2, Pallas kernels, half_tile(): pl.pallas_call(functools.partial(half_kernel, n), out_shape=jax.ShapeDtyp...  3.52 us
  transfers between devices with their start and end apart: 8, of which 5 were waited for; matrix products, arithmetic and copies ran while one was open for 0% of the time, Pallas kernels for 1%

profile of v2, /device:TPU:24, one launch (start us, length us, event | category | flops | bytes accessed | tf_op | source)
XLA Modules:
  0.0 104.4 jit_solution(11552838724835842818)
XLA Ops:
  3.9 1.4 %prepare.1 = (bf16[2,256,256]{2,1,0:T(8,128)(2,1)S(1)}, bf16[2,256,256]{2,1,0:T(8,128)(2,1)S(1)}, bf16[256,256]{1,0:T(8,128)(2,1)S(1)}, bf16[256,256]{1,0:T(8,128)(2,1)S(1)}, f32[256,128]{1,0:T(8,128)S(1)}) custom-call(f32[16,16]{1,0:T(8,128)} %bitcast.30, f32[128,128]{1,0:T(8,128)} %bitcast.29, f32[16,128]{1,0:T(8,128)} %bitcast.31), custom_call_target="tpu_custom_call" | custom-call | tf_op jit(solution)/shard_map/prepare/pallas_call | solution.py:76
  5.3 99.1 %conditional.1 = (f32[64,512]{1,0:T(8,128)}) conditional(s32[]{:T(128)} %clamp.3, (s32[1]{0:T(128)}, bf16[512,2048]{1,0:T(8,128)(2,1)}, bf16[2,256,256]{2,1,0:T(8,128)(2,1)S(1)}, bf16[2,256,256]{2,1,0:T(8,128)(2,1)S(1)}, bf16[256,256]{1,0:T(8,128)(2,1)S(1)}, /*index=5*/bf16[256,256]{1,0:T(8,128)(2,1)S(1)}, ...), branch_computations={%region_0.1_spmd, %region_1.2_spmd, %region_2.3_spmd, %region_3.4_... | conditional | flops 6442483712 | bytes 36569348 | solution.py:359
  5.5 6.8 %own.9.x = bf16[512,2048]{1,0:T(8,128)(2,1)S(1)} custom-call(s32[1]{0:T(128)} %get-tuple-element.145.lower, bf16[512,2048]{1,0:T(8,128)(2,1)} %get-tuple-element.146.x, bf16[2,256,256]{2,1,0:T(8,128)(2,1)S(1)} %get-tuple-element.147.lt, bf16[2,256,256]{2,1,0:T(8,128)(2,1)S(1)} %get-tuple-element.148.l, bf16[256,256]{1,0:T(8,128)(2,1)S(1)} %get-tuple-element.149.rr, ...), custom_call_target="tpu_custom_call" | custom-call | flops 5368709120 | bytes 4194304 | tf_op jit(solution)/shard_map/cond/branch_3_fun/own/pallas_call | solution.py:139
  12.3 0.3 piece.22
  12.6 1.9 %collective-permute-start.16 = (bf16[256,1024]{1,0:T(8,128)(2,1)S(1)}, bf16[256,1024]{1,0:T(8,128)(2,1)S(1)}, u32[]{:S(2)}, u32[]{:S(2)}) collective-permute-start(bf16[256,1024]{1,0:T(8,128)(2,1)S(1)} %piece.22), channel_id=1, source_target_pairs={{0,64},{8,72},{16,80},{24,88},{32,96},{40,104},{48,112},{56,120},{... | collective-permute-start | bytes 1572872 | tf_op jit(solution)/shard_map/cond/branch_3_fun/ppermute | solution.py:236
  14.5 13.6 %collective-permute-done.16.y.rest_0_ = bf16[256,1024]{1,0:T(8,128)(2,1)S(1)} collective-permute-done((bf16[256,1024]{1,0:T(8,128)(2,1)S(1)}, bf16[256,1024]{1,0:T(8,128)(2,1)S(1)}, u32[]{:S(2)}, u32[]{:S(2)}) %collective-permute-start.16) | collective-permute-done | bytes 524320 | tf_op jit(solution)/shard_map/cond/branch_3_fun/ppermute | solution.py:236
  28.1 0.8 half_tile.18
  28.9 1.0 copy-done.2
  29.9 4.7 %all-to-all-start.6 = ((f32[4,2,64,512]{3,2,1,0:T(8,128)}), f32[4,2,64,512]{3,2,1,0:T(8,128)S(1)}, u32[]{:S(2)}, u32[]{:S(2)}) async-start(f32[4,2,64,512]{3,2,1,0:T(8,128)} %bitcast.28), calls=%async_computation.6 | async-start | bytes 2097152 | tf_op jit(solution)/shard_map/cond/branch_3_fun/all_to_all | solution.py:230
  34.6 1.0 copy-done.8
  35.6 0.9 piece.23
  36.5 2.2 %collective-permute-start.19 = (bf16[256,1024]{1,0:T(8,128)(2,1)}, bf16[256,1024]{1,0:T(8,128)(2,1)}, u32[]{:S(2)}, u32[]{:S(2)}) collective-permute-start(bf16[256,1024]{1,0:T(8,128)(2,1)} %piece.23), channel_id=1, source_target_pairs={{0,64},{8,72},{16,80},{24,88},{32,96},{40,104},{48,112},{56,120},{... | collective-permute-start | bytes 1572872 | tf_op jit(solution)/shard_map/cond/branch_3_fun/ppermute | solution.py:236
  38.7 8.0 %all-to-all-done.6.parts = f32[4,2,64,512]{3,2,1,0:T(8,128)S(1)} async-done(((f32[4,2,64,512]{3,2,1,0:T(8,128)}), f32[4,2,64,512]{3,2,1,0:T(8,128)S(1)}, u32[]{:S(2)}, u32[]{:S(2)}) %all-to-all-start.6) | async-done | bytes 1048608 | tf_op jit(solution)/shard_map/cond/branch_3_fun/all_to_all | solution.py:230
  46.8 4.2 %collective-permute-done.19.y = bf16[256,1024]{1,0:T(8,128)(2,1)} collective-permute-done((bf16[256,1024]{1,0:T(8,128)(2,1)}, bf16[256,1024]{1,0:T(8,128)(2,1)}, u32[]{:S(2)}, u32[]{:S(2)}) %collective-permute-start.19) | collective-permute-done | bytes 524320 | tf_op jit(solution)/shard_map/cond/branch_3_fun/ppermute | solution.py:236
  50.9 2.8 %half_tile.19 = f32[8,64,512]{2,1,0:T(8,128)} custom-call(s32[1]{0:T(128)} %get-tuple-element.145.lower, bf16[256,1024]{1,0:T(8,128)(2,1)} %collective-permute-done.19.y, bf16[512,2048]{1,0:T(8,128)(2,1)S(1)} %own.9.x, f32[64,512]{1,0:T(8,128)S(1)} %get-tuple-element.152.rest_0_.refs_0_), custom_call_target="tpu_custom_call" | custom-call | flops 536870912 | bytes 3145728 | tf_op jit(solution)/shard_map/cond/branch_3_fun/half_tile/pallas_call | solution.py:293
  53.7 4.8 %all-to-all-start.7 = ((f32[4,2,64,512]{3,2,1,0:T(8,128)}), f32[4,2,64,512]{3,2,1,0:T(8,128)S(1)}, u32[]{:S(2)}, u32[]{:S(2)}) async-start(f32[4,2,64,512]{3,2,1,0:T(8,128)} %bitcast.7), calls=%async_computation.7 | async-start | bytes 2097152 | tf_op jit(solution)/shard_map/cond/branch_3_fun/all_to_all | solution.py:230
  58.5 15.7 %collective-permute-start.17 = (f32[64,512]{1,0:T(8,128)S(1)}, f32[64,512]{1,0:T(8,128)S(1)}, u32[]{:S(2)}, u32[]{:S(2)}) collective-permute-start(f32[64,512]{1,0:T(8,128)S(1)} %get-tuple-element.153), channel_id=1, source_target_pairs={{0,4},{1,5},{2,6},{3,7},{4,0},{5,1},{6,2},{7,3},{8,12},{9,13},{10,... | collective-permute-start | bytes 393224 | tf_op jit(solution)/shard_map/cond/branch_3_fun/ppermute | solution.py:232
  74.2 0.1 fold.23
  74.3 10.7 %collective-permute-start.20 = (f32[64,512]{1,0:T(8,128)S(1)}, f32[64,512]{1,0:T(8,128)S(1)}, u32[]{:S(2)}, u32[]{:S(2)}) collective-permute-start(f32[64,512]{1,0:T(8,128)S(1)} %get-tuple-element.155), channel_id=1, source_target_pairs={{0,4},{1,5},{2,6},{3,7},{4,0},{5,1},{6,2},{7,3},{8,12},{9,13},{10,... | collective-permute-start | bytes 393224 | tf_op jit(solution)/shard_map/cond/branch_3_fun/ppermute | solution.py:232
  85.0 2.8 %collective-permute-start.18 = (f32[32,512]{1,0:T(8,128)S(1)}, f32[32,512]{1,0:T(8,128)S(1)}, u32[]{:S(2)}, u32[]{:S(2)}) collective-permute-start(f32[32,512]{1,0:T(8,128)S(1)} %slice_add_fusion.5), channel_id=1, source_target_pairs={{0,64},{8,72},{16,80},{24,88},{32,96},{40,104},{48,112},{56,120},{... | collective-permute-start | bytes 196616 | tf_op jit(solution)/shard_map/cond/branch_3_fun/ppermute | solution.py:236
  87.8 9.6 %collective-permute-done.20.refs_4_ = f32[64,512]{1,0:T(8,128)S(1)} collective-permute-done((f32[64,512]{1,0:T(8,128)S(1)}, f32[64,512]{1,0:T(8,128)S(1)}, u32[]{:S(2)}, u32[]{:S(2)}) %collective-permute-start.20) | collective-permute-done | bytes 131104 | tf_op jit(solution)/shard_map/cond/branch_3_fun/ppermute | solution.py:232
  97.4 1.9 %collective-permute-start.21 = (f32[32,512]{1,0:T(8,128)S(1)}, f32[32,512]{1,0:T(8,128)S(1)}, u32[]{:S(2)}, u32[]{:S(2)}) collective-permute-start(f32[32,512]{1,0:T(8,128)S(1)} %slice_add_fusion.4), channel_id=1, source_target_pairs={{0,64},{8,72},{16,80},{24,88},{32,96},{40,104},{48,112},{56,120},{... | collective-permute-start | bytes 196616 | tf_op jit(solution)/shard_map/cond/branch_3_fun/ppermute | solution.py:236
  99.4 4.2 %collective-permute-done.21.refs_5_ = f32[32,512]{1,0:T(8,128)S(1)} collective-permute-done((f32[32,512]{1,0:T(8,128)S(1)}, f32[32,512]{1,0:T(8,128)S(1)}, u32[]{:S(2)}, u32[]{:S(2)}) %collective-permute-start.21) | collective-permute-done | bytes 65568 | tf_op jit(solution)/shard_map/cond/branch_3_fun/ppermute | solution.py:236
  103.6 0.8 last.7
  (10 shorter events, 0.1 us)
Async XLA Ops:
  12.6 15.5 %collective-permute-start.16 = (bf16[256,1024]{1,0:T(8,128)(2,1)S(1)}, bf16[256,1024]{1,0:T(8,128)(2,1)S(1)}, u32[]{:S(2)}, u32[]{:S(2)}) collective-permute-start(bf16[256,1024]{1,0:T(8,128)(2,1)S(1)} %piece.22), channel_id=1, source_target_pairs={{0,64},{8,72},{16,80},{24,88},{32,96},{40,104},{48,112},{56,120},{... | collective-permute-start | bytes 1572872 | tf_op jit(solution)/shard_map/cond/branch_3_fun/ppermute | solution.py:236
  28.1 0.8 copy-start.7
  28.9 1.0 copy-start.2
  29.9 16.8 %all-to-all-start.6 = ((f32[4,2,64,512]{3,2,1,0:T(8,128)}), f32[4,2,64,512]{3,2,1,0:T(8,128)S(1)}, u32[]{:S(2)}, u32[]{:S(2)}) async-start(f32[4,2,64,512]{3,2,1,0:T(8,128)} %bitcast.28), calls=%async_computation.6 | async-start | bytes 2097152 | tf_op jit(solution)/shard_map/cond/branch_3_fun/all_to_all | solution.py:230
  34.6 1.0 copy-start.8
  36.5 14.4 %collective-permute-start.19 = (bf16[256,1024]{1,0:T(8,128)(2,1)}, bf16[256,1024]{1,0:T(8,128)(2,1)}, u32[]{:S(2)}, u32[]{:S(2)}) collective-permute-start(bf16[256,1024]{1,0:T(8,128)(2,1)} %piece.23), channel_id=1, source_target_pairs={{0,64},{8,72},{16,80},{24,88},{32,96},{40,104},{48,112},{56,120},{... | collective-permute-start | bytes 1572872 | tf_op jit(solution)/shard_map/cond/branch_3_fun/ppermute | solution.py:236
  53.7 20.6 %all-to-all-start.7 = ((f32[4,2,64,512]{3,2,1,0:T(8,128)}), f32[4,2,64,512]{3,2,1,0:T(8,128)S(1)}, u32[]{:S(2)}, u32[]{:S(2)}) async-start(f32[4,2,64,512]{3,2,1,0:T(8,128)} %bitcast.7), calls=%async_computation.7 | async-start | bytes 2097152 | tf_op jit(solution)/shard_map/cond/branch_3_fun/all_to_all | solution.py:230
  58.5 26.5 %collective-permute-start.17 = (f32[64,512]{1,0:T(8,128)S(1)}, f32[64,512]{1,0:T(8,128)S(1)}, u32[]{:S(2)}, u32[]{:S(2)}) collective-permute-start(f32[64,512]{1,0:T(8,128)S(1)} %get-tuple-element.153), channel_id=1, source_target_pairs={{0,4},{1,5},{2,6},{3,7},{4,0},{5,1},{6,2},{7,3},{8,12},{9,13},{10,... | collective-permute-start | bytes 393224 | tf_op jit(solution)/shard_map/cond/branch_3_fun/ppermute | solution.py:232
  74.3 23.1 %collective-permute-start.20 = (f32[64,512]{1,0:T(8,128)S(1)}, f32[64,512]{1,0:T(8,128)S(1)}, u32[]{:S(2)}, u32[]{:S(2)}) collective-permute-start(f32[64,512]{1,0:T(8,128)S(1)} %get-tuple-element.155), channel_id=1, source_target_pairs={{0,4},{1,5},{2,6},{3,7},{4,0},{5,1},{6,2},{7,3},{8,12},{9,13},{10,... | collective-permute-start | bytes 393224 | tf_op jit(solution)/shard_map/cond/branch_3_fun/ppermute | solution.py:232
  85.0 14.3 %collective-permute-start.18 = (f32[32,512]{1,0:T(8,128)S(1)}, f32[32,512]{1,0:T(8,128)S(1)}, u32[]{:S(2)}, u32[]{:S(2)}) collective-permute-start(f32[32,512]{1,0:T(8,128)S(1)} %slice_add_fusion.5), channel_id=1, source_target_pairs={{0,64},{8,72},{16,80},{24,88},{32,96},{40,104},{48,112},{56,120},{... | collective-permute-start | bytes 196616 | tf_op jit(solution)/shard_map/cond/branch_3_fun/ppermute | solution.py:236
  97.4 6.2 %collective-permute-start.21 = (f32[32,512]{1,0:T(8,128)S(1)}, f32[32,512]{1,0:T(8,128)S(1)}, u32[]{:S(2)}, u32[]{:S(2)}) collective-permute-start(f32[32,512]{1,0:T(8,128)S(1)} %slice_add_fusion.4), channel_id=1, source_target_pairs={{0,64},{8,72},{16,80},{24,88},{32,96},{40,104},{48,112},{56,120},{... | collective-permute-start | bytes 196616 | tf_op jit(solution)/shard_map/cond/branch_3_fun/ppermute | solution.py:236

commit v3 on v1

v3 whole, which is shorter than its diff:
```python
import functools

import jax
import jax.numpy as jnp
from jax import lax
from jax.experimental import pallas as pl
from jax.experimental.pallas import tpu as pltpu
from jax.sharding import PartitionSpec as P

FA = 16
FB = 128
ROWS = 512
COLS = FA * FB
WIDE = 16 * FA
SHARE = 64
PAIRS = 4
HALF = COLS // 2
SCALE = 1.0 / 128.0
Y_GROUPS = [[0, 1, 2, 3], [4, 5, 6, 7]]
VMEM = pl.BlockSpec(memory_space=pltpu.VMEM)
SMEM = pl.BlockSpec(memory_space=pltpu.SMEM)
f32, bf16 = jnp.float32, jnp.bfloat16


def params(flops, moved, grant=28):
    return dict(
        compiler_params=pltpu.CompilerParams(vmem_limit_bytes=grant << 20),
        cost_estimate=pl.CostEstimate(flops=flops, bytes_accessed=moved, transcendentals=0),
    )


def split(v):
    high = v.astype(bf16)
    return high, (v - high.astype(f32)).astype(bf16)


def dot(a, b):
    return jnp.dot(a, b, preferred_element_type=f32)


def dot_t(a, b):
    return lax.dot_general(a, b, (((1,), (1,)), ((), ())), preferred_element_type=f32)


def prepare(left, right, eigen, lt, l, rr, rrt, inv):
    spread = (
        lax.broadcasted_iota(jnp.int32, (WIDE, FA), 0) >> 4
        == lax.broadcasted_iota(jnp.int32, (WIDE, FA), 1)
    ).astype(bf16)
    same = (lax.broadcasted_iota(jnp.int32, (WIDE, WIDE), 0) & 15) == (
        lax.broadcasted_iota(jnp.int32, (WIDE, WIDE), 1) & 15
    )
    for k, v in enumerate(split(left[...])):
        wide = dot_t(dot(spread, v).astype(bf16), spread)
        l[k] = jnp.where(same, wide, 0.0).astype(bf16)
        wide = dot_t(dot_t(spread, v).astype(bf16), spread)
        lt[k] = jnp.where(same, wide, 0.0).astype(bf16)
    for out, basis in ((rr, right[...]), (rrt, right[...].T)):
        for k, v in enumerate(split(basis)):
            out[:FB, k * FB : (k + 1) * FB] = v
            out[FB:, k * FB : (k + 1) * FB] = v
    reciprocal = 1.0 / (eigen[...] + 0.1)
    inv[...] = jnp.broadcast_to(reciprocal[:, None, :], (FA, 16, FB)).reshape(WIDE, FB)


PREPARED = (
    pltpu.VMEM((2, WIDE, WIDE), bf16),
    pltpu.VMEM((2, WIDE, WIDE), bf16),
    pltpu.VMEM((2 * FB, 2 * FB), bf16),
    pltpu.VMEM((2 * FB, 2 * FB), bf16),
    pltpu.VMEM((WIDE, FB), f32),
)


def halves(v):
    return v[:, :FB] + v[:, FB:]


def beside(v):
    return jnp.concatenate([v[:WIDE], v[WIDE:]], axis=1)


def precondition(x, store, lt, l, rr, rrt, inv):
    def some(g, carry):
        pairs = [
            [pl.ds(pl.multiple_of(((g * PAIRS + q) * 2 + k) * 16, 16), 16) for k in range(2)]
            for q in range(PAIRS)
        ]
        values = []
        for two in pairs:
            z = jnp.concatenate(
                [
                    jnp.concatenate([x[at, a * FB : (a + 1) * FB] for a in range(FA)], axis=0)
                    for at in two
                ],
                axis=1,
            )
            v = dot(lt[0], z) + dot(lt[1], z)
            values.append(jnp.concatenate([v[:, :FB], v[:, FB:]], axis=0))
        values = [halves(dot(jnp.concatenate(split(v), axis=1), rr[...])) for v in values]
        scale = jnp.concatenate([inv[...], inv[...]], axis=0)
        values = [v * scale for v in values]
        values = [halves(dot(jnp.concatenate(split(v), axis=1), rrt[...])) for v in values]
        for two, v in zip(pairs, values):
            high, low = [beside(part) for part in split(v)]
            v = (dot(l[0], high) + dot(l[1], high) + dot(l[0], low)).astype(bf16)
            for k, at in enumerate(two):
                for a in range(FA):
                    store(at, a, v[a * 16 : (a + 1) * 16, k * FB : (k + 1) * FB])
        return carry

    lax.fori_loop(0, x.shape[0] // (32 * PAIRS), some, 0)


def whole(a):
    return pl.BlockSpec(a.shape, lambda *_: (0,) * len(a.shape))


def own_kernel(me, partner, x, left, right, eigen, stays, leaves, *ready):
    lower = jnp.bitwise_and(me[0], partner[0, 0]) == 0

    @pl.when(lower)
    def _():
        @pl.when(pl.program_id(0) == 0)
        def _():
            prepare(left, right, eigen, *ready)

        def store(at, a, v):
            out, a = (stays, a) if a < FA // 2 else (leaves, a - FA // 2)
            out[at, a * FB : (a + 1) * FB] = v

        precondition(x, store, *ready)

    @pl.when(jnp.logical_not(lower))
    def _():
        stays[...] = x[:, HALF:]
        leaves[...] = x[:, :HALF]


def own_side(me, partner, x, left, right, eigen):
    step = 32 * PAIRS
    rows = pl.BlockSpec((step, HALF), lambda i: (i, 0))
    shape = jax.ShapeDtypeStruct((ROWS, HALF), bf16)
    return pl.pallas_call(
        own_kernel,
        grid=(ROWS // step,),
        out_shape=(shape, shape),
        in_specs=[SMEM, SMEM, pl.BlockSpec((step, COLS), lambda i: (i, 0))]
        + [whole(a) for a in (left, right, eigen)],
        out_specs=(rows, rows),
        scratch_shapes=PREPARED,
        name="own",
        **params(5 << 30, 4 << 20, 56),
    )(me, partner, x, left, right, eigen)


def tile_kernel(a, b, out):
    v = (dot_t(a[...], b[...]) * SCALE).astype(out.dtype)
    for i in range(8):
        first = ((i % 2) * 4 + i // 2) * SHARE
        out[i] = v[first : first + SHARE]


def tile(a, b):
    out = pl.pallas_call(
        tile_kernel,
        out_shape=jax.ShapeDtypeStruct((8, SHARE, ROWS), bf16),
        in_specs=[VMEM, VMEM],
        out_specs=VMEM,
        name="tile",
        **params(2 * ROWS * ROWS * HALF, 3 << 20),
    )(a, b)
    return out.reshape(4, 2, SHARE, ROWS)


def fold_kernel(parts, out):
    for z in range(2):
        four = [parts[y, z].astype(f32) for y in range(4)]
        out[z] = (four[0] + four[1]) + (four[2] + four[3])


def over_y(tile):
    parts = lax.all_to_all(tile, "feat", 0, 0, axis_index_groups=Y_GROUPS)
    return pl.pallas_call(
        fold_kernel,
        out_shape=jax.ShapeDtypeStruct((2, SHARE, ROWS), f32),
        in_specs=[VMEM],
        out_specs=VMEM,
        name="fold",
        **params(0, 4 * parts.size),
    )(parts)


def merge_kernel(z_hi, near, far, keep, send):
    z = z_hi[0]
    keep[...] = near[z] + far[z]
    send[...] = (near[1 - z] + far[1 - z]).astype(send.dtype)


def merge(z_hi, near, far):
    shape = (SHARE, ROWS)
    return pl.pallas_call(
        merge_kernel,
        out_shape=(jax.ShapeDtypeStruct(shape, f32), jax.ShapeDtypeStruct(shape, bf16)),
        in_specs=[SMEM, VMEM, VMEM],
        out_specs=(VMEM, VMEM),
        name="merge",
        **params(0, 4 * SHARE * ROWS * 6),
    )(z_hi, near, far)


def over_z(x):
    return lax.ppermute(x, "feat", [(f, f ^ 4) for f in range(8)])


def swap(level, x):
    def at(k):
        return lambda v: lax.ppermute(v, "blk", [(b, b ^ (1 << k)) for b in range(64)])

    return lax.switch(level, [at(k) for k in range(6)], x)


def body(grads, basis_left, basis_right, eigen, partner):
    mask = partner[0, 0]
    blk = lax.axis_index("blk").astype(jnp.int32).reshape(1)
    z_hi = (lax.axis_index("feat") // 4).astype(jnp.int32).reshape(1)
    level = sum((mask >= 1 << k).astype(jnp.int32) for k in range(1, 6))
    stays, leaves = own_side(
        blk, partner, grads, basis_left[0], basis_right[0], eigen.reshape(FA, FB)
    )
    arrived = swap(level, leaves)
    far = over_y(tile(stays, arrived))
    near = over_y(tile(arrived, stays))
    keep, send = merge(z_hi, near, swap(level, far))
    return (keep + over_z(send)).T[None]


def solution(mesh):
    placed = (P("blk", "feat"), P("feat", None, None), P("feat", None, None), P("feat"), P())
    return jax.shard_map(
        body, mesh=mesh, in_specs=placed, out_specs=P(None, "blk", "feat"), check_vma=False
    )
```

time: 132 us -> 67.7 us (0.51)
  the two profiles are of different devices: /device:TPU:34 before, /device:TPU:24 now
where the time goes in v3:
time: 67.7 us; the launch traced here: 66.4 us
  starting transfers between devices  29.2 us (43%)
  waiting for transfers between devices  17.2 us (25%)
  Pallas kernels  14.8 us (22%)
  between operations  3.27 us (5%)
  local copies, waits for them, and re-layouts  1.23 us (2%)
    all_to_all x2, starting transfers between devices, over_y(): parts = lax.all_to_all(tile, 'feat', 0, 0, axis_index_groups=Y_GROUPS)  14.6 us
    ppermute x1, starting transfers between devices, over_z(): return lax.ppermute(x, 'feat', [(f, f ^ 4) for f in range(8)])  10.8 us
    all_to_all x2, waiting for transfers between devices, over_y(): parts = lax.all_to_all(tile, 'feat', 0, 0, axis_index_groups=Y_GROUPS)  8.73 us
    pallas_call x1, Pallas kernels, own_side(): pl.pallas_call(own_kernel, grid=(ROWS // step,), out_shape=(shape, shape)...  8.08 us
    pallas_call x2, Pallas kernels, tile(): pl.pallas_call(tile_kernel, out_shape=jax.ShapeDtypeStruct((8, SHARE, ROW...  5.62 us
    ppermute x2, waiting for transfers between devices, at(): lax.ppermute(v, 'blk', [(b, b ^ 1 << k) for b in range(64)])  4.39 us
    ppermute x1, waiting for transfers between devices, over_z(): return lax.ppermute(x, 'feat', [(f, f ^ 4) for f in range(8)])  4.1 us
    ppermute x2, starting transfers between devices, at(): lax.ppermute(v, 'blk', [(b, b ^ 1 << k) for b in range(64)])  3.83 us
  transfers between devices with their start and end apart: 5, of which 5 were waited for; matrix products, arithmetic and copies ran while one was open for 0% of the time, Pallas kernels for 4%

profile of v3, /device:TPU:24, one launch (start us, length us, event | category | flops | bytes accessed | tf_op | source)
XLA Modules:
  0.0 66.4 jit_solution(11689545627477106900)
XLA Ops:
  3.2 8.1 %own.1 = (bf16[512,1024]{1,0:T(8,128)(2,1)}, bf16[512,1024]{1,0:T(8,128)(2,1)S(1)}) custom-call(s32[1]{0:T(128)} %bitcast.2.me, s32[1,64]{1,0:T(1,128)} %partner.1, bf16[512,2048]{1,0:T(8,128)(2,1)} %x.1, f32[16,16]{1,0:T(8,128)} %bitcast.14, f32[128,128]{1,0:T(8,128)} %bitcast.13, f32[16,128]{1,0:T(8,128)} %bitcast.15), custom_call_target="tpu_custom_call" | custom-call | flops 5368709120 | bytes 4194304 | tf_op jit(solution)/shard_map/own/pallas_call | solution.py:144
  11.3 4.7 %conditional.2 = (bf16[512,1024]{1,0:T(8,128)(2,1)}) conditional(s32[]{:T(128)} %bitcast.1, bf16[512,1024]{1,0:T(8,128)(2,1)S(1)} %get-tuple-element.35, bf16[512,1024]{1,0:T(8,128)(2,1)S(1)} %get-tuple-element.35, bf16[512,1024]{1,0:T(8,128)(2,1)S(1)} %get-tuple-element.35, ...), branch_computations={%region_0.1_spmd, %region_1.2_spmd, %region_2.3_spmd, %region_3.4_... | conditional | bytes 4194352 | solution.py:220
  11.3 1.9 %collective-permute-start = (bf16[512,1024]{1,0:T(8,128)(2,1)S(1)}, bf16[512,1024]{1,0:T(8,128)(2,1)}, u32[]{:S(2)}, u32[]{:S(2)}) collective-permute-start(bf16[512,1024]{1,0:T(8,128)(2,1)S(1)} %param), channel_id=1, source_target_pairs={{0,8},{8,0},{16,24},{24,16},{32,40},{40,32},{48,56},{56,48},{64,72... | collective-permute-start | bytes 3145736 | tf_op jit(solution)/shard_map/cond/branch_0_fun/ppermute | solution.py:218
  13.2 2.8 %collective-permute-done = bf16[512,1024]{1,0:T(8,128)(2,1)} collective-permute-done((bf16[512,1024]{1,0:T(8,128)(2,1)S(1)}, bf16[512,1024]{1,0:T(8,128)(2,1)}, u32[]{:S(2)}, u32[]{:S(2)}) %collective-permute-start) | collective-permute-done | bytes 1048608 | tf_op jit(solution)/shard_map/cond/branch_0_fun/ppermute | solution.py:218
  16.0 0.0 copy-start
  16.0 1.2 %copy-done = bf16[512,1024]{1,0:T(8,128)(2,1)S(1)} copy-done((bf16[512,1024]{1,0:T(8,128)(2,1)S(1)}, bf16[512,1024]{1,0:T(8,128)(2,1)}, u32[]{:S(2)}) %copy-start) | copy-done | bytes 1048600
  17.2 0.0 copy-start.1
  17.2 2.8 %tile.3 = bf16[8,64,512]{2,1,0:T(8,128)(2,1)} custom-call(bf16[512,1024]{1,0:T(8,128)(2,1)S(1)} %copy-done, bf16[512,1024]{1,0:T(8,128)(2,1)} %get-tuple-element.39.a.b), custom_call_target="tpu_custom_call" | custom-call | flops 536870912 | bytes 3145728 | tf_op jit(solution)/shard_map/tile/pallas_call | solution.py:165
  20.1 9.1 %all-to-all-start.1 = ((bf16[4,2,64,512]{3,2,1,0:T(8,128)(2,1)}), bf16[4,2,64,512]{3,2,1,0:T(8,128)(2,1)S(1)}, u32[]{:S(2)}, u32[]{:S(2)}) async-start(bf16[4,2,64,512]{3,2,1,0:T(8,128)(2,1)} %bitcast.7), calls=%async_computation.1 | async-start | bytes 1048576 | tf_op jit(solution)/shard_map/all_to_all | solution.py:183
  29.1 0.0 copy-done.1
  29.1 2.8 %tile.2 = bf16[8,64,512]{2,1,0:T(8,128)(2,1)} custom-call(bf16[512,1024]{1,0:T(8,128)(2,1)} %get-tuple-element.39.a.b, bf16[512,1024]{1,0:T(8,128)(2,1)S(1)} %copy-done.1), custom_call_target="tpu_custom_call" | custom-call | flops 536870912 | bytes 3145728 | tf_op jit(solution)/shard_map/tile/pallas_call | solution.py:165
  31.9 5.2 %all-to-all-done.1.parts = bf16[4,2,64,512]{3,2,1,0:T(8,128)(2,1)S(1)} async-done(((bf16[4,2,64,512]{3,2,1,0:T(8,128)(2,1)}), bf16[4,2,64,512]{3,2,1,0:T(8,128)(2,1)S(1)}, u32[]{:S(2)}, u32[]{:S(2)}) %all-to-all-start.1) | async-done | bytes 524320 | tf_op jit(solution)/shard_map/all_to_all | solution.py:183
  37.1 5.5 %all-to-all-start = ((bf16[4,2,64,512]{3,2,1,0:T(8,128)(2,1)}), bf16[4,2,64,512]{3,2,1,0:T(8,128)(2,1)S(1)}, u32[]{:S(2)}, u32[]{:S(2)}) async-start(bf16[4,2,64,512]{3,2,1,0:T(8,128)(2,1)} %bitcast.6), calls=%async_computation | async-start | bytes 1048576 | tf_op jit(solution)/shard_map/all_to_all | solution.py:183
  42.6 0.1 fold.3
  42.7 3.6 %conditional.3 = (f32[2,64,512]{2,1,0:T(8,128)}) conditional(s32[]{:T(128)} %bitcast.1, f32[2,64,512]{2,1,0:T(8,128)S(1)} %fold.3, f32[2,64,512]{2,1,0:T(8,128)S(1)} %fold.3, f32[2,64,512]{2,1,0:T(8,128)S(1)} %fold.3, f32[2,64,512]{2,1,0:T(8,128)S(1)} %fold.3, f32[2,64,512]{2,1,0:T(8,128)S(1)} %fold.3, ...), branch_computations={%region_6.7_spmd, %region_7.8_spmd, %region_8.9_spmd, %region_9.10... | conditional | bytes 1048624 | solution.py:220
  42.7 1.9 %collective-permute-start.6 = (f32[2,64,512]{2,1,0:T(8,128)S(1)}, f32[2,64,512]{2,1,0:T(8,128)}, u32[]{:S(2)}, u32[]{:S(2)}) collective-permute-start(f32[2,64,512]{2,1,0:T(8,128)S(1)} %param.6), channel_id=1, source_target_pairs={{0,8},{8,0},{16,24},{24,16},{32,40},{40,32},{48,56},{56,48},{64,72... | collective-permute-start | bytes 786440 | tf_op jit(solution)/shard_map/cond/branch_0_fun/ppermute | solution.py:218
  44.6 1.6 %collective-permute-done.6 = f32[2,64,512]{2,1,0:T(8,128)} collective-permute-done((f32[2,64,512]{2,1,0:T(8,128)S(1)}, f32[2,64,512]{2,1,0:T(8,128)}, u32[]{:S(2)}, u32[]{:S(2)}) %collective-permute-start.6) | collective-permute-done | bytes 262176 | tf_op jit(solution)/shard_map/cond/branch_0_fun/ppermute | solution.py:218
  46.3 3.5 %all-to-all-done.parts = bf16[4,2,64,512]{3,2,1,0:T(8,128)(2,1)S(1)} async-done(((bf16[4,2,64,512]{3,2,1,0:T(8,128)(2,1)}), bf16[4,2,64,512]{3,2,1,0:T(8,128)(2,1)S(1)}, u32[]{:S(2)}, u32[]{:S(2)}) %all-to-all-start) | async-done | bytes 524320 | tf_op jit(solution)/shard_map/all_to_all | solution.py:183
  49.8 0.1 fold.2.near
  49.9 1.0 %merge.1 = (f32[64,512]{1,0:T(8,128)S(1)}, bf16[64,512]{1,0:T(8,128)(2,1)S(1)}) custom-call(s32[1]{0:T(128)} %bitcast.z_hi, f32[2,64,512]{2,1,0:T(8,128)S(1)} %fold.2.near, f32[2,64,512]{2,1,0:T(8,128)} %get-tuple-element.40.far), custom_call_target="tpu_custom_call" | custom-call | bytes 786432 | tf_op jit(solution)/shard_map/merge/pallas_call | solution.py:202
  50.8 10.8 %collective-permute-start.12 = (bf16[64,512]{1,0:T(8,128)(2,1)S(1)}, bf16[64,512]{1,0:T(8,128)(2,1)S(1)}, u32[]{:S(2)}, u32[]{:S(2)}) collective-permute-start(bf16[64,512]{1,0:T(8,128)(2,1)S(1)} %get-tuple-element.38), channel_id=1, source_target_pairs={{0,4},{1,5},{2,6},{3,7},{4,0},{5,1},{6,2},{7,3},{8,12},{9,13},{10,... | collective-permute-start | bytes 196616 | tf_op jit(solution)/shard_map/ppermute | solution.py:213
  61.6 4.1 %collective-permute-done.12 = bf16[64,512]{1,0:T(8,128)(2,1)S(1)} collective-permute-done((bf16[64,512]{1,0:T(8,128)(2,1)S(1)}, bf16[64,512]{1,0:T(8,128)(2,1)S(1)}, u32[]{:S(2)}, u32[]{:S(2)}) %collective-permute-start.12) | collective-permute-done | bytes 65568 | tf_op jit(solution)/shard_map/ppermute | solution.py:213
  65.7 0.7 %add_bitcast_fusion = f32[1,512,64]{1,2,0:T(8,128)} fusion(f32[64,512]{1,0:T(8,128)S(1)} %get-tuple-element.37, bf16[64,512]{1,0:T(8,128)(2,1)S(1)} %collective-permute-done.12), kind=kLoop, calls=%fused_computation | loop fusion | flops 65536 | bytes 327680 | tf_op jit(solution)/shard_map/broadcast_in_dim | solution.py:235
Async XLA Ops:
  11.3 4.7 %collective-permute-start = (bf16[512,1024]{1,0:T(8,128)(2,1)S(1)}, bf16[512,1024]{1,0:T(8,128)(2,1)}, u32[]{:S(2)}, u32[]{:S(2)}) collective-permute-start(bf16[512,1024]{1,0:T(8,128)(2,1)S(1)} %param), channel_id=1, source_target_pairs={{0,8},{8,0},{16,24},{24,16},{32,40},{40,32},{48,56},{56,48},{64,72... | collective-permute-start | bytes 3145736 | tf_op jit(solution)/shard_map/cond/branch_0_fun/ppermute | solution.py:218
  16.0 1.2 %copy-start = (bf16[512,1024]{1,0:T(8,128)(2,1)S(1)}, bf16[512,1024]{1,0:T(8,128)(2,1)}, u32[]{:S(2)}) copy-start(bf16[512,1024]{1,0:T(8,128)(2,1)} %get-tuple-element.36.b.a) | copy-start | bytes 3145732
  17.2 11.9 %copy-start.1 = (bf16[512,1024]{1,0:T(8,128)(2,1)S(1)}, bf16[512,1024]{1,0:T(8,128)(2,1)}, u32[]{:S(2)}) copy-start(bf16[512,1024]{1,0:T(8,128)(2,1)} %get-tuple-element.36.b.a) | copy-start | bytes 3145732
  20.1 17.0 %all-to-all-start.1 = ((bf16[4,2,64,512]{3,2,1,0:T(8,128)(2,1)}), bf16[4,2,64,512]{3,2,1,0:T(8,128)(2,1)S(1)}, u32[]{:S(2)}, u32[]{:S(2)}) async-start(bf16[4,2,64,512]{3,2,1,0:T(8,128)(2,1)} %bitcast.7), calls=%async_computation.1 | async-start | bytes 1048576 | tf_op jit(solution)/shard_map/all_to_all | solution.py:183
  37.1 12.7 %all-to-all-start = ((bf16[4,2,64,512]{3,2,1,0:T(8,128)(2,1)}), bf16[4,2,64,512]{3,2,1,0:T(8,128)(2,1)S(1)}, u32[]{:S(2)}, u32[]{:S(2)}) async-start(bf16[4,2,64,512]{3,2,1,0:T(8,128)(2,1)} %bitcast.6), calls=%async_computation | async-start | bytes 1048576 | tf_op jit(solution)/shard_map/all_to_all | solution.py:183
  42.7 3.6 %collective-permute-start.6 = (f32[2,64,512]{2,1,0:T(8,128)S(1)}, f32[2,64,512]{2,1,0:T(8,128)}, u32[]{:S(2)}, u32[]{:S(2)}) collective-permute-start(f32[2,64,512]{2,1,0:T(8,128)S(1)} %param.6), channel_id=1, source_target_pairs={{0,8},{8,0},{16,24},{24,16},{32,40},{40,32},{48,56},{56,48},{64,72... | collective-permute-start | bytes 786440 | tf_op jit(solution)/shard_map/cond/branch_0_fun/ppermute | solution.py:218
  50.8 14.9 %collective-permute-start.12 = (bf16[64,512]{1,0:T(8,128)(2,1)S(1)}, bf16[64,512]{1,0:T(8,128)(2,1)S(1)}, u32[]{:S(2)}, u32[]{:S(2)}) collective-permute-start(bf16[64,512]{1,0:T(8,128)(2,1)S(1)} %get-tuple-element.38), channel_id=1, source_target_pairs={{0,4},{1,5},{2,6},{3,7},{4,0},{5,1},{6,2},{7,3},{8,12},{9,13},{10,... | collective-permute-start | bytes 196616 | tf_op jit(solution)/shard_map/ppermute | solution.py:213

commit v4 on v3

--- a/solution.py
+++ b/solution.py
@@ -154,23 +154,51 @@
     )(me, partner, x, left, right, eigen)
 
 
-def tile_kernel(a, b, out):
-    v = (dot_t(a[...], b[...]) * SCALE).astype(out.dtype)
+def shares(v, out):
     for i in range(8):
         first = ((i % 2) * 4 + i // 2) * SHARE
-        out[i] = v[first : first + SHARE]
-
-
-def tile(a, b):
+        out[i] = v[first : first + SHARE].astype(out.dtype)
+
+
+TILE = jax.ShapeDtypeStruct((8, SHARE, ROWS), bf16)
+
+
+def ordered(tile):
+    return tile.reshape(4, 2, SHARE, ROWS)
+
+
+def both_kernel(arrived, stays, near, far):
+    v = dot_t(arrived[...], stays[...]) * SCALE
+    shares(v.T, far)
+    shares(v, near)
+
+
+def both_tiles(arrived, stays):
+    near, far = pl.pallas_call(
+        both_kernel,
+        out_shape=(TILE, TILE),
+        in_specs=[VMEM, VMEM],
+        out_specs=(VMEM, VMEM),
+        name="both_tiles",
+        **params(2 * ROWS * ROWS * HALF, 4 << 20, 56),
+    )(arrived, stays)
+    return ordered(near), ordered(far)
+
+
+def full_kernel(first, stays, second, leaves, out):
+    shares((dot_t(first[...], stays[...]) + dot_t(second[...], leaves[...])) * SCALE, out)
+
+
+def full_tile(first, stays, second, leaves):
     out = pl.pallas_call(
-        tile_kernel,
-        out_shape=jax.ShapeDtypeStruct((8, SHARE, ROWS), bf16),
-        in_specs=[VMEM, VMEM],
+        full_kernel,
+        out_shape=TILE,
+        in_specs=[VMEM] * 4,
         out_specs=VMEM,
-        name="tile",
-        **params(2 * ROWS * ROWS * HALF, 3 << 20),
-    )(a, b)
-    return out.reshape(4, 2, SHARE, ROWS)
+        name="full_tile",
+        **params(4 * ROWS * ROWS * HALF, 5 << 20, 56),
+    )(first, stays, second, leaves)
+    return ordered(out)
 
 
 def fold_kernel(parts, out):
@@ -191,22 +219,25 @@
     )(parts)
 
 
-def merge_kernel(z_hi, near, far, keep, send):
-    z = z_hi[0]
-    keep[...] = near[z] + far[z]
-    send[...] = (near[1 - z] + far[1 - z]).astype(send.dtype)
+def merge_kernel(z_hi, *refs):
+    sums, (keep, send) = refs[:-2], refs[-2:]
+    for z, out in ((z_hi[0], keep), (1 - z_hi[0], send)):
+        v = sums[0][z]
+        for more in sums[1:]:
+            v = v + more[z]
+        out[...] = v.astype(out.dtype)
 
 
 def merge(z_hi, near, far):
-    shape = (SHARE, ROWS)
+    sums, shape = [near] if far is None else [near, far], (SHARE, ROWS)
     return pl.pallas_call(
         merge_kernel,
         out_shape=(jax.ShapeDtypeStruct(shape, f32), jax.ShapeDtypeStruct(shape, bf16)),
-        in_specs=[SMEM, VMEM, VMEM],
+        in_specs=[SMEM] + [VMEM] * len(sums),
         out_specs=(VMEM, VMEM),
         name="merge",
         **params(0, 4 * SHARE * ROWS * 6),
-    )(z_hi, near, far)
+    )(z_hi, *sums)
 
 
 def over_z(x):
@@ -214,10 +245,21 @@
 
 
 def swap(level, x):
-    def at(k):
-        return lambda v: lax.ppermute(v, "blk", [(b, b ^ (1 << k)) for b in range(64)])
-
-    return lax.switch(level, [at(k) for k in range(6)], x)
+    return lax.ppermute(x, "blk", [(b, b ^ (1 << level)) for b in range(64)])
+
+
+def swap_far(level, x):
+    return lax.switch(level - 1, [functools.partial(swap, k) for k in range(1, 6)], x)
+
+
+def by_blocks(level, stays, leaves):
+    return over_y(full_tile(swap(0, leaves), stays, swap(0, stays), leaves)), None
+
+
+def by_halves(level, stays, leaves):
+    near, far = both_tiles(swap_far(level, leaves), stays)
+    far = over_y(far)
+    return over_y(near), swap_far(level, far)
 
 
 def body(grads, basis_left, basis_right, eigen, partner):
@@ -228,10 +270,14 @@
     stays, leaves = own_side(
         blk, partner, grads, basis_left[0], basis_right[0], eigen.reshape(FA, FB)
     )
-    arrived = swap(level, leaves)
-    far = over_y(tile(stays, arrived))
-    near = over_y(tile(arrived, stays))
-    keep, send = merge(z_hi, near, swap(level, far))
+    keep, send = lax.cond(
+        level == 0,
+        lambda *args: merge(z_hi, *by_blocks(*args)),
+        lambda *args: merge(z_hi, *by_halves(*args)),
+        level,
+        stays,
+        leaves,
+    )
     return (keep + over_z(send)).T[None]
 
 

time: 67.7 us -> 86.6 us (1.28)
  waiting for transfers between devices: 17.2 us -> 33.3 us
  blocking collectives: 0 us -> 11.2 us
  starting transfers between devices: 29.2 us -> 25.7 us
  Pallas kernels: 14.8 us -> 11.4 us
  local copies, waits for them, and re-layouts: 1.23 us -> 0 us
    ppermute x2, waiting for transfers between devices: 4.39 us -> 30.8 us  [swap(): return lax.ppermute(x, 'blk', [(b, b ^ 1 << level) for b in range(64)])]
    all_to_all x0 -> x1, blocking collectives: none -> 11.2 us  [over_y(): parts = lax.all_to_all(tile, 'feat', 0, 0, axis_index_groups=Y_GROUPS)]
    all_to_all x2 -> x1, starting transfers between devices: 14.6 us -> 5.51 us  [over_y(): parts = lax.all_to_all(tile, 'feat', 0, 0, axis_index_groups=Y_GROUPS)]
    all_to_all x2 -> x1, waiting for transfers between devices: 8.73 us -> 0.01 us  [over_y(): parts = lax.all_to_all(tile, 'feat', 0, 0, axis_index_groups=Y_GROUPS)]
    ppermute x1, starting transfers between devices: 10.8 us -> 15.7 us  [over_z(): return lax.ppermute(x, 'feat', [(f, f ^ 4) for f in range(8)])]
    pallas_call x2 -> x1, Pallas kernels: 5.62 us -> 2.95 us  [both_tiles(): pl.pallas_call(both_kernel, out_shape=(TILE, TILE), in_specs=[VMEM, VMEM]...]
    ppermute x1, waiting for transfers between devices: 4.1 us -> 2.52 us  [over_z(): return lax.ppermute(x, 'feat', [(f, f ^ 4) for f in range(8)])]
    unnamed x4 -> x0, local copies, waits for them, and re-layouts: 1.23 us -> none
  transfers between devices with their start and end apart: 5 -> 4, of which waited for: 5 -> 3; matrix products, arithmetic and copies ran while one was open for 0% -> 0% of each run, Pallas kernels for 4% -> 0%
where the time goes in v4:
time: 86.6 us; the launch traced here: 85.7 us
  waiting for transfers between devices  33.3 us (38%)
  starting transfers between devices  25.7 us (30%)
  Pallas kernels  11.4 us (13%)
  blocking collectives  11.2 us (13%)
  between operations  3.28 us (4%)
    ppermute x2, waiting for transfers between devices, swap(): return lax.ppermute(x, 'blk', [(b, b ^ 1 << level) for b in range(64)])  30.8 us
    ppermute x1, starting transfers between devices, over_z(): return lax.ppermute(x, 'feat', [(f, f ^ 4) for f in range(8)])  15.7 us
    all_to_all x1, blocking collectives, over_y(): parts = lax.all_to_all(tile, 'feat', 0, 0, axis_index_groups=Y_GROUPS)  11.2 us
    pallas_call x1, Pallas kernels, own_side(): pl.pallas_call(own_kernel, grid=(ROWS // step,), out_shape=(shape, shape)...  7.38 us
    all_to_all x1, starting transfers between devices, over_y(): parts = lax.all_to_all(tile, 'feat', 0, 0, axis_index_groups=Y_GROUPS)  5.51 us
    ppermute x2, starting transfers between devices, swap(): return lax.ppermute(x, 'blk', [(b, b ^ 1 << level) for b in range(64)])  4.44 us
    pallas_call x1, Pallas kernels, both_tiles(): pl.pallas_call(both_kernel, out_shape=(TILE, TILE), in_specs=[VMEM, VMEM]...  2.95 us
    ppermute x1, waiting for transfers between devices, over_z(): return lax.ppermute(x, 'feat', [(f, f ^ 4) for f in range(8)])  2.52 us
  transfers between devices with their start and end apart: 4, of which 3 were waited for; matrix products, arithmetic and copies ran while one was open for 0% of the time, Pallas kernels for 0%

profile of v4, /device:TPU:24, one launch (start us, length us, event | category | flops | bytes accessed | tf_op | source)
XLA Modules:
  0.0 85.7 jit_solution(7629311736876830327)
XLA Ops:
  3.3 7.4 %own.1 = (bf16[512,1024]{1,0:T(8,128)(2,1)S(1)}, bf16[512,1024]{1,0:T(8,128)(2,1)S(1)}) custom-call(s32[1]{0:T(128)} %bitcast.4.me, s32[1,64]{1,0:T(1,128)} %partner.1, bf16[512,2048]{1,0:T(8,128)(2,1)} %x.1, f32[16,16]{1,0:T(8,128)} %bitcast.18, f32[128,128]{1,0:T(8,128)} %bitcast.17, f32[16,128]{1,0:T(8,128)} %bitcast.19), custom_call_target="tpu_custom_call" | custom-call | flops 5368709120 | bytes 4194304 | tf_op jit(solution)/shard_map/own/pallas_call | solution.py:144
  10.6 56.1 %conditional.3 = ((f32[64,512]{1,0:T(8,128)S(1)}, bf16[64,512]{1,0:T(8,128)(2,1)S(1)})) conditional(s32[]{:T(128)} %convert_element_type.37, (s32[]{:T(128)}, bf16[512,1024]{1,0:T(8,128)(2,1)S(1)}, bf16[512,1024]{1,0:T(8,128)(2,1)S(1)}, s32[1]{0:T(128)}) %tuple.41, (bf16[512,1024]{1,0:T(8,128)(2,1)S(1)}, bf16[512,1024]{1,0:T(8,128)(2,1)S(1)}, ...), branch_computations={%region_0.11_spmd, %region_11.12_spmd} | conditional | flops 1073741824 | bytes 24903824 | solution.py:273
  10.7 26.9 %conditional = (bf16[512,1024]{1,0:T(8,128)(2,1)}) conditional(s32[]{:T(128)} %clamp.0, bf16[512,1024]{1,0:T(8,128)(2,1)S(1)} %get-tuple-element.43, bf16[512,1024]{1,0:T(8,128)(2,1)S(1)} %get-tuple-element.43, bf16[512,1024]{1,0:T(8,128)(2,1)S(1)} %get-tuple-element.43, ...), branch_computations={%region_1.1_spmd, %region_2.2_spmd, %region_3.3_spmd, %region_4.4_... | conditional | bytes 4194352 | solution.py:252
  10.7 1.9 %collective-permute-start = (bf16[512,1024]{1,0:T(8,128)(2,1)S(1)}, bf16[512,1024]{1,0:T(8,128)(2,1)}, u32[]{:S(2)}, u32[]{:S(2)}) collective-permute-start(bf16[512,1024]{1,0:T(8,128)(2,1)S(1)} %param), channel_id=1, source_target_pairs={{0,16},{8,24},{16,0},{24,8},{32,48},{40,56},{48,32},{56,40},{64,80... | collective-permute-start | bytes 3145736 | tf_op jit(solution)/shard_map/cond/branch_0_fun/cond/branch_0_fun/ppermute | solution.py:248
  12.6 25.0 %collective-permute-done = bf16[512,1024]{1,0:T(8,128)(2,1)} collective-permute-done((bf16[512,1024]{1,0:T(8,128)(2,1)S(1)}, bf16[512,1024]{1,0:T(8,128)(2,1)}, u32[]{:S(2)}, u32[]{:S(2)}) %collective-permute-start) | collective-permute-done | bytes 1048608 | tf_op jit(solution)/shard_map/cond/branch_0_fun/cond/branch_0_fun/ppermute | solution.py:248
  37.6 3.0 %both_tiles.1 = (bf16[8,64,512]{2,1,0:T(8,128)(2,1)}, bf16[8,64,512]{2,1,0:T(8,128)(2,1)}) custom-call(bf16[512,1024]{1,0:T(8,128)(2,1)} %get-tuple-element.62.arrived, bf16[512,1024]{1,0:T(8,128)(2,1)S(1)} %get-tuple-element.44.stays), custom_call_target="tpu_custom_call" | custom-call | flops 536870912 | bytes 4194304 | tf_op jit(solution)/shard_map/cond/branch_0_fun/both_tiles/pallas_call | solution.py:177
  40.5 11.2 %all_to_all.12.parts = bf16[4,2,64,512]{3,2,1,0:T(8,128)(2,1)S(1)} all-to-all(bf16[4,2,64,512]{3,2,1,0:T(8,128)(2,1)} %bitcast.16), channel_id=1, replica_groups={{0,1,2,3},{4,5,6,7},{8,9,10,11},{12,13,14,15},{16,17,18,19},{20,21,22,2..., dimensions={0} | all-to-all | bytes 1048576 | tf_op jit(solution)/shard_map/cond/branch_0_fun/all_to_all | solution.py:211
  51.8 5.5 %all-to-all-start = ((bf16[4,2,64,512]{3,2,1,0:T(8,128)(2,1)}), bf16[4,2,64,512]{3,2,1,0:T(8,128)(2,1)S(1)}, u32[]{:S(2)}, u32[]{:S(2)}) async-start(bf16[4,2,64,512]{3,2,1,0:T(8,128)(2,1)} %bitcast.15), calls=%async_computation | async-start | bytes 1048576 | tf_op jit(solution)/shard_map/cond/branch_0_fun/all_to_all | solution.py:211
  57.3 0.1 fold.4
  57.3 8.4 %conditional.1 = (f32[2,64,512]{2,1,0:T(8,128)}) conditional(s32[]{:T(128)} %clamp.0, f32[2,64,512]{2,1,0:T(8,128)S(1)} %fold.4, f32[2,64,512]{2,1,0:T(8,128)S(1)} %fold.4, f32[2,64,512]{2,1,0:T(8,128)S(1)} %fold.4, f32[2,64,512]{2,1,0:T(8,128)S(1)} %fold.4, f32[2,64,512]{2,1,0:T(8,128)S(1)} %fold.4), branch_computations={%region_6.6_spmd, %region_7.7_spmd, %region_8.8_spmd, %region_9.9_... | conditional | bytes 1048624 | solution.py:252
  57.3 2.5 %collective-permute-start.5 = (f32[2,64,512]{2,1,0:T(8,128)S(1)}, f32[2,64,512]{2,1,0:T(8,128)}, u32[]{:S(2)}, u32[]{:S(2)}) collective-permute-start(f32[2,64,512]{2,1,0:T(8,128)S(1)} %param.5), channel_id=1, source_target_pairs={{0,16},{8,24},{16,0},{24,8},{32,48},{40,56},{48,32},{56,40},{64,80... | collective-permute-start | bytes 786440 | tf_op jit(solution)/shard_map/cond/branch_0_fun/cond/branch_0_fun/ppermute | solution.py:248
  59.9 5.8 %collective-permute-done.5 = f32[2,64,512]{2,1,0:T(8,128)} collective-permute-done((f32[2,64,512]{2,1,0:T(8,128)S(1)}, f32[2,64,512]{2,1,0:T(8,128)}, u32[]{:S(2)}, u32[]{:S(2)}) %collective-permute-start.5) | collective-permute-done | bytes 262176 | tf_op jit(solution)/shard_map/cond/branch_0_fun/cond/branch_0_fun/ppermute | solution.py:248
  65.7 0.0 all-to-all-done.parts
  65.7 0.1 fold.3.refs_0_
  65.8 1.0 %merge.2 = (f32[64,512]{1,0:T(8,128)S(1)}, bf16[64,512]{1,0:T(8,128)(2,1)S(1)}) custom-call(s32[1]{0:T(128)} %get-tuple-element.41.z_hi, f32[2,64,512]{2,1,0:T(8,128)S(1)} %fold.3.refs_0_, f32[2,64,512]{2,1,0:T(8,128)} %get-tuple-element.63.refs_1_), custom_call_target="tpu_custom_call" | custom-call | bytes 786432 | tf_op jit(solution)/shard_map/cond/branch_0_fun/merge/pallas_call | solution.py:233
  66.8 15.7 %collective-permute-start.12 = (bf16[64,512]{1,0:T(8,128)(2,1)S(1)}, bf16[64,512]{1,0:T(8,128)(2,1)S(1)}, u32[]{:S(2)}, u32[]{:S(2)}) collective-permute-start(bf16[64,512]{1,0:T(8,128)(2,1)S(1)} %get-tuple-element.57), channel_id=1, source_target_pairs={{0,4},{1,5},{2,6},{3,7},{4,0},{5,1},{6,2},{7,3},{8,12},{9,13},{10,... | collective-permute-start | bytes 196616 | tf_op jit(solution)/shard_map/ppermute | solution.py:244
  82.5 2.5 %collective-permute-done.12 = bf16[64,512]{1,0:T(8,128)(2,1)S(1)} collective-permute-done((bf16[64,512]{1,0:T(8,128)(2,1)S(1)}, bf16[64,512]{1,0:T(8,128)(2,1)S(1)}, u32[]{:S(2)}, u32[]{:S(2)}) %collective-permute-start.12) | collective-permute-done | bytes 65568 | tf_op jit(solution)/shard_map/ppermute | solution.py:244
  85.0 0.7 add_bitcast_fusion
Async XLA Ops:
  10.7 26.9 %collective-permute-start = (bf16[512,1024]{1,0:T(8,128)(2,1)S(1)}, bf16[512,1024]{1,0:T(8,128)(2,1)}, u32[]{:S(2)}, u32[]{:S(2)}) collective-permute-start(bf16[512,1024]{1,0:T(8,128)(2,1)S(1)} %param), channel_id=1, source_target_pairs={{0,16},{8,24},{16,0},{24,8},{32,48},{40,56},{48,32},{56,40},{64,80... | collective-permute-start | bytes 3145736 | tf_op jit(solution)/shard_map/cond/branch_0_fun/cond/branch_0_fun/ppermute | solution.py:248
  51.8 14.0 %all-to-all-start = ((bf16[4,2,64,512]{3,2,1,0:T(8,128)(2,1)}), bf16[4,2,64,512]{3,2,1,0:T(8,128)(2,1)S(1)}, u32[]{:S(2)}, u32[]{:S(2)}) async-start(bf16[4,2,64,512]{3,2,1,0:T(8,128)(2,1)} %bitcast.15), calls=%async_computation | async-start | bytes 1048576 | tf_op jit(solution)/shard_map/cond/branch_0_fun/all_to_all | solution.py:211
  57.3 8.4 %collective-permute-start.5 = (f32[2,64,512]{2,1,0:T(8,128)S(1)}, f32[2,64,512]{2,1,0:T(8,128)}, u32[]{:S(2)}, u32[]{:S(2)}) collective-permute-start(f32[2,64,512]{2,1,0:T(8,128)S(1)} %param.5), channel_id=1, source_target_pairs={{0,16},{8,24},{16,0},{24,8},{32,48},{40,56},{48,32},{56,40},{64,80... | collective-permute-start | bytes 786440 | tf_op jit(solution)/shard_map/cond/branch_0_fun/cond/branch_0_fun/ppermute | solution.py:248
  66.8 18.3 %collective-permute-start.12 = (bf16[64,512]{1,0:T(8,128)(2,1)S(1)}, bf16[64,512]{1,0:T(8,128)(2,1)S(1)}, u32[]{:S(2)}, u32[]{:S(2)}) collective-permute-start(bf16[64,512]{1,0:T(8,128)(2,1)S(1)} %get-tuple-element.57), channel_id=1, source_target_pairs={{0,4},{1,5},{2,6},{3,7},{4,0},{5,1},{6,2},{7,3},{8,12},{9,13},{10,... | collective-permute-start | bytes 196616 | tf_op jit(solution)/shard_map/ppermute | solution.py:244

commit v5 on v4

--- a/solution.py
+++ b/solution.py
@@ -155,16 +155,17 @@
 
 
 def shares(v, out):
+    rows = v.shape[0] // 8
     for i in range(8):
-        first = ((i % 2) * 4 + i // 2) * SHARE
-        out[i] = v[first : first + SHARE].astype(out.dtype)
+        first = ((i % 2) * 4 + i // 2) * rows
+        out[i] = v[first : first + rows].astype(out.dtype)
 
 
 TILE = jax.ShapeDtypeStruct((8, SHARE, ROWS), bf16)
 
 
 def ordered(tile):
-    return tile.reshape(4, 2, SHARE, ROWS)
+    return tile.reshape(4, 2, *tile.shape[1:])
 
 
 def both_kernel(arrived, stays, near, far):
@@ -211,7 +212,7 @@
     parts = lax.all_to_all(tile, "feat", 0, 0, axis_index_groups=Y_GROUPS)
     return pl.pallas_call(
         fold_kernel,
-        out_shape=jax.ShapeDtypeStruct((2, SHARE, ROWS), f32),
+        out_shape=jax.ShapeDtypeStruct(parts.shape[1:], f32),
         in_specs=[VMEM],
         out_specs=VMEM,
         name="fold",
@@ -228,8 +229,8 @@
         out[...] = v.astype(out.dtype)
 
 
-def merge(z_hi, near, far):
-    sums, shape = [near] if far is None else [near, far], (SHARE, ROWS)
+def merge(z_hi, *sums):
+    shape = (SHARE, ROWS)
     return pl.pallas_call(
         merge_kernel,
         out_shape=(jax.ShapeDtypeStruct(shape, f32), jax.ShapeDtypeStruct(shape, bf16)),
@@ -248,36 +249,30 @@
     return lax.ppermute(x, "blk", [(b, b ^ (1 << level)) for b in range(64)])
 
 
-def swap_far(level, x):
+def swap_along(level, x):
     return lax.switch(level - 1, [functools.partial(swap, k) for k in range(1, 6)], x)
 
 
-def by_blocks(level, stays, leaves):
-    return over_y(full_tile(swap(0, leaves), stays, swap(0, stays), leaves)), None
-
-
-def by_halves(level, stays, leaves):
-    near, far = both_tiles(swap_far(level, leaves), stays)
+def by_blocks(level, z_hi, stays, leaves):
+    tile = full_tile(swap(0, leaves), stays, swap(0, stays), leaves)
+    return merge(z_hi, over_y(tile))
+
+
+def by_halves(level, z_hi, stays, leaves):
+    near, far = both_tiles(swap_along(level, leaves), stays)
     far = over_y(far)
-    return over_y(near), swap_far(level, far)
+    return merge(z_hi, over_y(near), swap_along(level, far))
 
 
 def body(grads, basis_left, basis_right, eigen, partner):
     mask = partner[0, 0]
     blk = lax.axis_index("blk").astype(jnp.int32).reshape(1)
-    z_hi = (lax.axis_index("feat") // 4).astype(jnp.int32).reshape(1)
-    level = sum((mask >= 1 << k).astype(jnp.int32) for k in range(1, 6))
+    z_hi = (lax.axis_index("feat") >> 2).astype(jnp.int32).reshape(1)
+    level = lax.population_count(mask - 1)
     stays, leaves = own_side(
         blk, partner, grads, basis_left[0], basis_right[0], eigen.reshape(FA, FB)
     )
-    keep, send = lax.cond(
-        level == 0,
-        lambda *args: merge(z_hi, *by_blocks(*args)),
-        lambda *args: merge(z_hi, *by_halves(*args)),
-        level,
-        stays,
-        leaves,
-    )
+    keep, send = lax.cond(level == 0, by_blocks, by_halves, level, z_hi, stays, leaves)
     return (keep + over_z(send)).T[None]
 
 

time: 86.6 us -> 170 us (1.96)
  waiting for transfers between devices: 33.3 us -> 114 us
  starting transfers between devices: 25.7 us -> 30.6 us
  between operations: 3.28 us -> 0.69 us
    ppermute x2, waiting for transfers between devices: 30.8 us -> 112 us  [swap(): return lax.ppermute(x, 'blk', [(b, b ^ 1 << level) for b in range(64)])]
    ppermute x1, starting transfers between devices: 15.7 us -> 18.9 us  [over_z(): return lax.ppermute(x, 'feat', [(f, f ^ 4) for f in range(8)])]
where the time goes in v5:
time: 170 us; the launch traced here: 169 us
  waiting for transfers between devices  114 us (67%)
  starting transfers between devices  30.6 us (18%)
  Pallas kernels  11.4 us (7%)
  blocking collectives  11.2 us (7%)
    ppermute x2, waiting for transfers between devices, swap(): return lax.ppermute(x, 'blk', [(b, b ^ 1 << level) for b in range(64)])  112 us
    ppermute x1, starting transfers between devices, over_z(): return lax.ppermute(x, 'feat', [(f, f ^ 4) for f in range(8)])  18.9 us
    all_to_all x1, blocking collectives, over_y(): parts = lax.all_to_all(tile, 'feat', 0, 0, axis_index_groups=Y_GROUPS)  11.2 us
    pallas_call x1, Pallas kernels, own_side(): pl.pallas_call(own_kernel, grid=(ROWS // step,), out_shape=(shape, shape)...  7.38 us
    ppermute x2, starting transfers between devices, swap(): return lax.ppermute(x, 'blk', [(b, b ^ 1 << level) for b in range(64)])  6.14 us
    all_to_all x1, starting transfers between devices, over_y(): parts = lax.all_to_all(tile, 'feat', 0, 0, axis_index_groups=Y_GROUPS)  5.51 us
  transfers between devices with their start and end apart: 4, of which 3 were waited for; matrix products, arithmetic and copies ran while one was open for 0% of the time, Pallas kernels for 0%

profile of v5, /device:TPU:24, one launch (start us, length us, event | category | flops | bytes accessed | tf_op | source)
XLA Modules:
  0.0 169.0 jit_solution(10660251154272985419)
XLA Ops:
  0.7 7.4 %own.1 = (bf16[512,1024]{1,0:T(8,128)(2,1)S(1)}, bf16[512,1024]{1,0:T(8,128)(2,1)S(1)}) custom-call(s32[1]{0:T(128)} %bitcast.4.me, s32[1,64]{1,0:T(1,128)} %partner.1, bf16[512,2048]{1,0:T(8,128)(2,1)} %x.1, f32[16,16]{1,0:T(8,128)} %bitcast.18, f32[128,128]{1,0:T(8,128)} %bitcast.17, f32[16,128]{1,0:T(8,128)} %bitcast.19), custom_call_target="tpu_custom_call" | custom-call | flops 5368709120 | bytes 4194304 | tf_op jit(solution)/shard_map/own/pallas_call | solution.py:144
  8.1 139.1 %conditional.3 = ((f32[64,512]{1,0:T(8,128)S(1)}, bf16[64,512]{1,0:T(8,128)(2,1)S(1)})) conditional(s32[]{:T(128)} %convert_element_type.6, (s32[]{:T(128)}, bf16[512,1024]{1,0:T(8,128)(2,1)S(1)}, bf16[512,1024]{1,0:T(8,128)(2,1)S(1)}, s32[1]{0:T(128)}) %tuple.41, (bf16[512,1024]{1,0:T(8,128)(2,1)S(1)}, bf16[512,1024]{1,0:T(8,128)(2,1)S(1)}, ...), branch_computations={%region_0.0_spmd, %region_11.0_spmd} | conditional | flops 1073741824 | bytes 24903824 | solution.py:275
  8.1 98.2 %conditional = (bf16[512,1024]{1,0:T(8,128)(2,1)}) conditional(s32[]{:T(128)} %clamp.0, bf16[512,1024]{1,0:T(8,128)(2,1)S(1)} %get-tuple-element.43, bf16[512,1024]{1,0:T(8,128)(2,1)S(1)} %get-tuple-element.43, bf16[512,1024]{1,0:T(8,128)(2,1)S(1)} %get-tuple-element.43, ...), branch_computations={%region_1.0_spmd, %region_2.0_spmd, %region_3.0_spmd, %region_4.0_... | conditional | bytes 4194352 | solution.py:253
  8.1 4.2 %collective-permute-start.4 = (bf16[512,1024]{1,0:T(8,128)(2,1)S(1)}, bf16[512,1024]{1,0:T(8,128)(2,1)}, u32[]{:S(2)}, u32[]{:S(2)}) collective-permute-start(bf16[512,1024]{1,0:T(8,128)(2,1)S(1)} %param.4), channel_id=1, source_target_pairs={{0,256},{8,264},{16,272},{24,280},{32,288},{40,296},{48,304},{56,3... | collective-permute-start | bytes 3145736 | tf_op jit(solution)/shard_map/cond/branch_0_fun/cond/branch_4_fun/ppermute | solution.py:249
  12.3 94.0 %collective-permute-done.4 = bf16[512,1024]{1,0:T(8,128)(2,1)} collective-permute-done((bf16[512,1024]{1,0:T(8,128)(2,1)S(1)}, bf16[512,1024]{1,0:T(8,128)(2,1)}, u32[]{:S(2)}, u32[]{:S(2)}) %collective-permute-start.4) | collective-permute-done | bytes 1048608 | tf_op jit(solution)/shard_map/cond/branch_0_fun/cond/branch_4_fun/ppermute | solution.py:249
  106.3 3.0 %both_tiles.1 = (bf16[8,64,512]{2,1,0:T(8,128)(2,1)}, bf16[8,64,512]{2,1,0:T(8,128)(2,1)}) custom-call(bf16[512,1024]{1,0:T(8,128)(2,1)} %get-tuple-element.62.arrived, bf16[512,1024]{1,0:T(8,128)(2,1)S(1)} %get-tuple-element.44.stays), custom_call_target="tpu_custom_call" | custom-call | flops 536870912 | bytes 4194304 | tf_op jit(solution)/shard_map/cond/branch_0_fun/both_tiles/pallas_call | solution.py:178
  109.3 11.2 %all_to_all.12.parts = bf16[4,2,64,512]{3,2,1,0:T(8,128)(2,1)S(1)} all-to-all(bf16[4,2,64,512]{3,2,1,0:T(8,128)(2,1)} %bitcast.16), channel_id=1, replica_groups={{0,1,2,3},{4,5,6,7},{8,9,10,11},{12,13,14,15},{16,17,18,19},{20,21,22,2..., dimensions={0} | all-to-all | bytes 1048576 | tf_op jit(solution)/shard_map/cond/branch_0_fun/all_to_all | solution.py:212
  120.5 5.5 %all-to-all-start = ((bf16[4,2,64,512]{3,2,1,0:T(8,128)(2,1)}), bf16[4,2,64,512]{3,2,1,0:T(8,128)(2,1)S(1)}, u32[]{:S(2)}, u32[]{:S(2)}) async-start(bf16[4,2,64,512]{3,2,1,0:T(8,128)(2,1)} %bitcast.15), calls=%async_computation | async-start | bytes 1048576 | tf_op jit(solution)/shard_map/cond/branch_0_fun/all_to_all | solution.py:212
  126.0 0.1 fold.4
  126.1 20.1 %conditional.1 = (f32[2,64,512]{2,1,0:T(8,128)}) conditional(s32[]{:T(128)} %clamp.0, f32[2,64,512]{2,1,0:T(8,128)S(1)} %fold.4, f32[2,64,512]{2,1,0:T(8,128)S(1)} %fold.4, f32[2,64,512]{2,1,0:T(8,128)S(1)} %fold.4, f32[2,64,512]{2,1,0:T(8,128)S(1)} %fold.4, f32[2,64,512]{2,1,0:T(8,128)S(1)} %fold.4), branch_computations={%region_6.0_spmd, %region_7.0_spmd, %region_8.0_spmd, %region_9.0_... | conditional | bytes 1048624 | solution.py:253
  126.1 1.9 %collective-permute-start.9 = (f32[2,64,512]{2,1,0:T(8,128)S(1)}, f32[2,64,512]{2,1,0:T(8,128)}, u32[]{:S(2)}, u32[]{:S(2)}) collective-permute-start(f32[2,64,512]{2,1,0:T(8,128)S(1)} %param.9), channel_id=1, source_target_pairs={{0,256},{8,264},{16,272},{24,280},{32,288},{40,296},{48,304},{56,3... | collective-permute-start | bytes 786440 | tf_op jit(solution)/shard_map/cond/branch_0_fun/cond/branch_4_fun/ppermute | solution.py:249
  128.0 18.1 %collective-permute-done.9 = f32[2,64,512]{2,1,0:T(8,128)} collective-permute-done((f32[2,64,512]{2,1,0:T(8,128)S(1)}, f32[2,64,512]{2,1,0:T(8,128)}, u32[]{:S(2)}, u32[]{:S(2)}) %collective-permute-start.9) | collective-permute-done | bytes 262176 | tf_op jit(solution)/shard_map/cond/branch_0_fun/cond/branch_4_fun/ppermute | solution.py:249
  146.1 0.0 all-to-all-done.parts
  146.1 0.1 fold.3.refs_0_
  146.2 1.0 merge.2
  147.2 18.9 %collective-permute-start.12 = (bf16[64,512]{1,0:T(8,128)(2,1)S(1)}, bf16[64,512]{1,0:T(8,128)(2,1)S(1)}, u32[]{:S(2)}, u32[]{:S(2)}) collective-permute-start(bf16[64,512]{1,0:T(8,128)(2,1)S(1)} %get-tuple-element.57), channel_id=1, source_target_pairs={{0,4},{1,5},{2,6},{3,7},{4,0},{5,1},{6,2},{7,3},{8,12},{9,13},{10,... | collective-permute-start | bytes 196616 | tf_op jit(solution)/shard_map/ppermute | solution.py:245
  166.1 2.2 %collective-permute-done.12 = bf16[64,512]{1,0:T(8,128)(2,1)S(1)} collective-permute-done((bf16[64,512]{1,0:T(8,128)(2,1)S(1)}, bf16[64,512]{1,0:T(8,128)(2,1)S(1)}, u32[]{:S(2)}, u32[]{:S(2)}) %collective-permute-start.12) | collective-permute-done | bytes 65568 | tf_op jit(solution)/shard_map/ppermute | solution.py:245
  168.4 0.7 add_bitcast_fusion
Async XLA Ops:
  8.1 98.2 %collective-permute-start.4 = (bf16[512,1024]{1,0:T(8,128)(2,1)S(1)}, bf16[512,1024]{1,0:T(8,128)(2,1)}, u32[]{:S(2)}, u32[]{:S(2)}) collective-permute-start(bf16[512,1024]{1,0:T(8,128)(2,1)S(1)} %param.4), channel_id=1, source_target_pairs={{0,256},{8,264},{16,272},{24,280},{32,288},{40,296},{48,304},{56,3... | collective-permute-start | bytes 3145736 | tf_op jit(solution)/shard_map/cond/branch_0_fun/cond/branch_4_fun/ppermute | solution.py:249
  120.5 25.6 %all-to-all-start = ((bf16[4,2,64,512]{3,2,1,0:T(8,128)(2,1)}), bf16[4,2,64,512]{3,2,1,0:T(8,128)(2,1)S(1)}, u32[]{:S(2)}, u32[]{:S(2)}) async-start(bf16[4,2,64,512]{3,2,1,0:T(8,128)(2,1)} %bitcast.15), calls=%async_computation | async-start | bytes 1048576 | tf_op jit(solution)/shard_map/cond/branch_0_fun/all_to_all | solution.py:212
  126.1 20.0 %collective-permute-start.9 = (f32[2,64,512]{2,1,0:T(8,128)S(1)}, f32[2,64,512]{2,1,0:T(8,128)}, u32[]{:S(2)}, u32[]{:S(2)}) collective-permute-start(f32[2,64,512]{2,1,0:T(8,128)S(1)} %param.9), channel_id=1, source_target_pairs={{0,256},{8,264},{16,272},{24,280},{32,288},{40,296},{48,304},{56,3... | collective-permute-start | bytes 786440 | tf_op jit(solution)/shard_map/cond/branch_0_fun/cond/branch_4_fun/ppermute | solution.py:249
  147.2 21.2 %collective-permute-start.12 = (bf16[64,512]{1,0:T(8,128)(2,1)S(1)}, bf16[64,512]{1,0:T(8,128)(2,1)S(1)}, u32[]{:S(2)}, u32[]{:S(2)}) collective-permute-start(bf16[64,512]{1,0:T(8,128)(2,1)S(1)} %get-tuple-element.57), channel_id=1, source_target_pairs={{0,4},{1,5},{2,6},{3,7},{4,0},{5,1},{6,2},{7,3},{8,12},{9,13},{10,... | collective-permute-start | bytes 196616 | tf_op jit(solution)/shard_map/ppermute | solution.py:245
